TPU v7x, 128 devices: a whole 4x4x4 slice. The times are simulated.
128 devices in a mesh: shard: 8 (over x_lo, y), replica: 16 (over z, x_hi, core).
Axes of the slice: x: 4 (x_hi: 2, x_lo: 2; x = x_hi * 2 + x_lo), y: 4, z: 4, core: 2. Of those that a mesh axis runs over, the one named last changes fastest.
Arguments:
- tokens: bfloat16 [16, 2048, 1024], P('replica', 'shard'), may hold values from -6 to 6
- norm_in: bfloat16 [1024], P('shard'), may hold values from 0.5 to 1.5
- w_in: bfloat16 [1024, 3072], P('shard'), may hold values from -0.1875 to 0.1875
- conv_w: bfloat16 [1024, 3], P('shard'), may hold values from -3 to 3
- w_out: bfloat16 [1024, 1024], P('shard'), may hold values from -0.1875 to 0.1875
- norm_mid: bfloat16 [1024], P('shard'), may hold values from 0.5 to 1.5
- w_gate: bfloat16 [1024, 4608], P('shard'), may hold values from -0.1875 to 0.1875
- w_up: bfloat16 [1024, 4608], P('shard'), may hold values from -0.1875 to 0.1875
- w_down: bfloat16 [1024, 4608], P('shard'), may hold values from -0.09375 to 0.09375
- cotangent: bfloat16 [16, 2048, 1024], P('replica', 'shard'), may hold values from -6 to 6
Outputs:
- result: bfloat16 [16, 2048, 1024], P('replica', 'shard')
- grad_tokens: float32 [16, 2048, 1024], P('replica', 'shard')
- grad_norm_in: float32 [1024], P('shard')
- grad_w_in: float32 [1024, 3072], P('shard')
- grad_conv_w: float32 [1024, 3], P('shard')
- grad_w_out: float32 [1024, 1024], P('shard')
- grad_norm_mid: float32 [1024], P('shard')
- grad_w_gate: float32 [1024, 4608], P('shard')
- grad_w_up: float32 [1024, 4608], P('shard')
- grad_w_down: float32 [1024, 4608], P('shard')
All inputs are finite; a program needn't handle non-finite values.
Results may differ from a plain program's by a relative error of at most 0.011.
Values may be sent and summed in bfloat16 or wider, within the bound.
A program may use at most 256 MiB of HBM per device.

v0:
```python
import jax
import jax.numpy as jnp
from jax import lax
from jax.sharding import PartitionSpec as P
from jax.experimental import pallas as pl
from jax.experimental.pallas import tpu as pltpu

MESH = pl.DeviceIdType.MESH
BF = jnp.bfloat16
F32 = jnp.float32
EPS = 1e-05


def place():
    s = lax.axis_index("shard")
    r = lax.axis_index("replica")
    xl, y = s // 4, s % 4
    z, xh, c = r // 4, (r // 2) % 2, r % 2
    return xl, xh, y, z, c


def device(x, y, z, c):
    x, y, z = (x + 4) % 4, (y + 4) % 4, (z + 4) % 4
    return ((x % 2) * 4 + y, z * 4 + (x // 2) * 2 + c)


def remote(src, dst, send, recv, to):
    return pltpu.make_async_remote_copy(
        src_ref=src, dst_ref=dst, send_sem=send, recv_sem=recv, device_id=to, device_id_type=MESH
    )


def greet(devices):
    barrier = pltpu.get_barrier_semaphore()
    for to in devices:
        pl.semaphore_signal(barrier, inc=1, device_id=to, device_id_type=MESH)
    pl.semaphore_wait(barrier, len(devices))


def mul(left, right):
    return lax.dot_general(left, right, (((1,), (0,)), ((), ())), preferred_element_type=F32)


def times_rows(left, right):
    return lax.dot_general(left, right, (((1,), (1,)), ((), ())), preferred_element_type=F32)


def normalize(values):
    scale = lax.rsqrt(jnp.mean(values * values, axis=-1, keepdims=True) + EPS)
    return values * scale, scale


def norm_back(grad_normed, normed, scale):
    return scale * (grad_normed - normed * jnp.mean(grad_normed * normed, axis=-1, keepdims=True))


def loop(count, body):
    def step(i, carry):
        body(i)
        return carry

    lax.fori_loop(0, count, step, 0)


def chunk(i, size):
    return pl.ds(pl.multiple_of(i * size, size), size)


def flat(value):
    return value.reshape(-1, value.shape[-1])


SWAPS = ("tokens", "cot", "gated0", "gated1", "mix", "act", "ffn", "gam", "gmix", "gai", "fore", "back")
TILE = 256


def block_kernel(
    tokens, cot, w_in, w_out, w_gate, w_up, w_down, gains, taps_in,
    result, grad_tokens, o_act_in, o_act_mid, o_hidden, o_gg, o_gu, o_proj, o_gated, o_mix, o_cot, o_small,
    win, wout, wgu, wd, ext, tok2, cot2, act_in, proj, mixed, conv, gated, part, box_mix, box_ffn, box_gam, box_gai,
    resid, normed, act_mid, hidden, fac_a, fac_b, gg, gu, gmix, gconv, gproj, vecs, small, scale_mid, out_res,
    local_sem, send_sem, recv_sem, core_send, core_recv, out_sem,
):
    xl, xh, y, z, c = place()
    x = xh * 2 + xl
    shard, replica = lax.axis_index("shard"), lax.axis_index("replica")
    own = xl * 4 + y
    length, width = tokens.shape
    half = width // 2
    ff = wd.shape[2]
    rows = wd.shape[1]
    mine = z % 2
    xp, xm = device(x + 1, y, z, c), device(x - 1, y, z, c)
    yp, ym = device(x, y + 1, z, c), device(x, y - 1, z, c)
    zp, zm = device(x, y, z + 1, c), device(x, y, z - 1, c)
    sibling = device(x, y, z, 1 - c)
    nxt, prv = ((shard + 1) % 8, replica), ((shard + 7) % 8, replica)
    first, last = shard == 0, shard == 7

    ext[own] = jnp.concatenate([gains[...].astype(F32), taps_in[...].astype(F32), jnp.zeros((27, 128), F32)], axis=0).astype(BF)
    copies = []
    for i in range(3):
        copies.append((w_in.at[:, pl.ds(pl.multiple_of(i * width + c * half, 128), half)], win.at[own, :, pl.ds(i * half, half)]))
    copies.append((w_gate.at[:, pl.ds(pl.multiple_of(c * ff, 128), ff)], wgu.at[0, own]))
    copies.append((w_up.at[:, pl.ds(pl.multiple_of(c * ff, 128), ff)], wgu.at[1, own]))
    copies.append((w_out, wout.at[own]))
    copies.append((w_down.at[:, pl.ds(pl.multiple_of(c * ff, 128), ff)], wd.at[own]))
    copies.append((tokens, tok2.at[pl.ds(0, length)]))
    copies.append((cot, cot2.at[pl.ds(0, length)]))
    loads = [pltpu.make_async_copy(a, b, local_sem.at[i]) for i, (a, b) in enumerate(copies)]
    for cp in loads:
        cp.start()
    greet([xp, xm, yp, ym, zp, zm, sibling, nxt, prv])

    pending = []

    def fire(cp):
        cp.start()
        pending.append(cp.wait_send)

    def swap(name, src, dst, to=None):
        k = SWAPS.index(name)
        return remote(src, dst, core_send.at[k], core_recv.at[k], sibling if to is None else to)

    def wd_part(g, u):
        return wd.at[u, pl.ds(pl.multiple_of(g * (rows // 2), rows // 2), rows // 2)]

    parts = [
        (lambda g, u: ext.at[u], False),
        (lambda g, u: win.at[u], False),
        (lambda g, u: wgu.at[g, u], True),
        (lambda g, u: wout.at[u], False),
        (wd_part, True),
    ]
    keys, count = {}, 0
    for p in range(len(parts)):
        names = ["y+", "y-", "f+", "f-"]
        for dy in (0, -1, 1, 2):
            for h in (0, 1):
                names.append(("x", dy, h))
                if parts[p][1]:
                    names.append(("z", 1, dy, h))
                    if dy:
                        names.append(("z", 0, dy, h))
        for name in names:
            keys[p, name] = count
            count += 1
    assert count == COPIES

    def send(view, to, k):
        fire(remote(view, view, send_sem.at[k], recv_sem.at[k], to))

    def got(view, k):
        remote(view, view, send_sem.at[k], recv_sem.at[k], yp).wait_recv()

    def cut(view, h):
        hr = view.shape[0] // 2
        return view.at[pl.ds(h * hr, hr)]

    def at_y(dy):
        return xl * 4 + (y + dy + 4) % 4

    def over(dy):
        return (1 - xl) * 4 + (y + dy + 4) % 4

    def send_x(p, dy, h):
        send(cut(parts[p][0](mine, at_y(dy)), h), (xp, xm)[h], keys[p, ("x", dy, h)])

    def send_z(p, other, dy, h):
        if parts[p][1]:
            u = over(dy) if other else at_y(dy)
            send(cut(parts[p][0](mine, u), h), (zp, zm)[h], keys[p, ("z", other, dy, h)])

    def launch(p):
        view = parts[p][0]
        send(view(mine, own), yp, keys[p, "y+"])
        send(view(mine, own), ym, keys[p, "y-"])
        for h in (0, 1):
            send_x(p, 0, h)

    def stage_a(p):
        view = parts[p][0]
        got(view(mine, at_y(-1)), keys[p, "y+"])
        send(cut(view(mine, at_y(-1)), 0), yp, keys[p, "f+"])
        for h in (0, 1):
            send_z(p, 0, -1, h)
            send_x(p, -1, h)
        got(view(mine, at_y(1)), keys[p, "y-"])
        send(cut(view(mine, at_y(1)), 1), ym, keys[p, "f-"])
        for h in (0, 1):
            send_z(p, 0, 1, h)
            send_x(p, 1, h)

    def stage_b(p):
        view = parts[p][0]
        for h in (0, 1):
            got(cut(view(mine, at_y(2)), h), keys[p, ("f+", "f-")[h]])
            send_z(p, 0, 2, h)
            send_x(p, 2, h)

    def stage_c(p, dys=(0, -1, 1, 2)):
        view = parts[p][0]
        for dy in dys:
            for h in (0, 1):
                got(cut(view(mine, over(dy)), h), keys[p, ("x", dy, h)])
                send_z(p, 1, dy, h)

    def stage_d(p):
        view = parts[p][0]
        for h in (0, 1):
            for dy in (0, -1, 1, 2):
                if dy:
                    got(cut(view(1 - mine, at_y(dy)), h), keys[p, ("z", 0, dy, h)])
                got(cut(view(1 - mine, over(dy)), h), keys[p, ("z", 1, dy, h)])

    EXT, WIN, WGU, WOUT, WD = range(5)
    lower, upper = pl.ds(0, length), pl.ds(length, length)
    launch(EXT)
    for cp in loads[:3]:
        cp.wait()
    launch(WIN)
    for cp in loads[3:5]:
        cp.wait()
    launch(WGU)
    for cp in loads[7:]:
        cp.wait()
    fire(swap("tokens", tok2.at[lower], tok2.at[upper]))
    fire(swap("cot", cot2.at[lower], cot2.at[upper]))
    for cp in loads[5:7]:
        cp.wait()
    launch(WOUT)
    launch(WD)
    for stage in (stage_a, stage_b, stage_c):
        stage(EXT)
    for u in range(8):
        vecs[:, pl.ds(u * 128, 128)] = ext[u, pl.ds(0, 16)].astype(F32)
    small[...] = jnp.zeros_like(small)
    mixed[:, pl.ds(0, 8)] = jnp.zeros((2, 8, half), F32)
    gconv[:, pl.ds(length, 8)] = jnp.zeros((2, 8, half), F32)
    stage_a(WIN)
    swap("tokens", tok2.at[lower], tok2.at[upper]).wait_recv()
    rc = 32

    def norm_in_step(i):
        v, _ = normalize(tok2[chunk(i, rc)].astype(F32))
        act_in[chunk(i, rc)] = (v * vecs[0:1]).astype(BF)

    loop(2 * length // rc, norm_in_step)
    stage_b(WIN)
    stage_a(WGU)
    stage_c(WIN)

    def proj_step(j):
        proj[:, chunk(j, TILE)] = mul(act_in[...], flat(win[:, :, chunk(j, TILE)]))

    loop(3 * half // TILE, proj_step)

    def b_of(at):
        return proj[at, pl.ds(0, half)]

    def c_of(at):
        return proj[at, pl.ds(half, half)]

    def x_of(at):
        return proj[at, pl.ds(2 * half, half)]

    def mixed_step(i):
        for q in (0, 1):
            at = pl.ds(pl.multiple_of(q * length + i * rc, rc), rc)
            mixed[q, pl.ds(pl.multiple_of(8 + i * rc, 8), rc)] = (b_of(at) * x_of(at)).astype(BF).astype(F32)

    loop(length // rc, mixed_step)
    fore = swap("fore", mixed.at[:, pl.ds(length, 8)], mixed.at[:, pl.ds(0, 8)], nxt)
    back = swap("back", gconv.at[:, pl.ds(0, 8)], gconv.at[:, pl.ds(length, 8)], prv)

    @pl.when(jnp.logical_not(last))
    def _():
        fore.start()

    stage_b(WGU)

    @pl.when(jnp.logical_not(first))
    def _():
        fore.wait_recv()

    taps = [vecs[pl.ds(2 + k, 1), pl.ds(pl.multiple_of(c * half, 128), half)] for k in range(3)]
    rq = 64

    def conv_step(i):
        for q in (0, 1):
            window = mixed[q, pl.ds(pl.multiple_of(i * rq, 8), rq + 8)]
            value = taps[0] * window[6 : 6 + rq] + taps[1] * window[7 : 7 + rq] + taps[2] * window[8 : 8 + rq]
            at = pl.ds(pl.multiple_of(q * length + i * rq, rq), rq)
            conv[at] = value
            gated[at, pl.ds(pl.multiple_of(c * half, 128), half)] = (c_of(at) * value).astype(BF)

    loop(length // rq, conv_step)
    gated_mine = gated.at[:, pl.ds(pl.multiple_of(c * half, 128), half)]
    gated_other = gated.at[:, pl.ds(pl.multiple_of((1 - c) * half, 128), half)]
    fire(swap("gated0", gated_mine.at[lower], gated_mine.at[upper]))
    fire(swap("gated1", gated_mine.at[upper], gated_mine.at[lower]))
    for stage in (stage_a, stage_b, stage_c):
        stage(WOUT)
    wout_mine = wout.at[pl.ds(pl.multiple_of(c * 4, 4), 4)]

    def mix_step(j):
        part[:, chunk(j, TILE)] = mul(gated_mine[...], flat(wout_mine[:, :, chunk(j, TILE)]))

    loop(width // TILE, mix_step)
    mix_swap = swap("mix", part.at[upper], box_mix)
    mix_swap.start()
    stage_c(WGU, (0, -1))
    mix_swap.wait_recv()

    def norm_mid_step(i):
        at = chunk(i, rc)
        v = tok2[at].astype(F32) + part[at] + box_mix[at]
        n, s = normalize(v)
        resid[at] = v
        normed[at] = n
        scale_mid[at] = jnp.broadcast_to(s, (rc, 128))
        act_mid[at] = (n * vecs[1:2]).astype(BF)

    loop(length // rc, norm_mid_step)
    act_swap = swap("act", act_mid.at[lower], act_mid.at[upper])
    act_swap.start()
    stage_c(WGU, (1, 2))
    stage_a(WD)
    act_swap.wait_recv()
    stage_b(WD)
    stage_c(WD)
    stage_d(WGU)

    def gate_step(j):
        at = chunk(j, TILE)
        gate = mul(act_mid[...], flat(wgu[0, :, :, at]))
        up = mul(act_mid[...], flat(wgu[1, :, :, at]))
        sig = jax.nn.sigmoid(gate)
        silu = gate * sig
        hidden[:, at] = (silu * up).astype(BF)
        fac_b[:, at] = silu
        fac_a[:, at] = up * (sig * (1.0 + gate * (1.0 - sig)))

    loop(ff // TILE, gate_step)
    stage_d(WD)
    swap("cot", cot2.at[lower], cot2.at[upper]).wait_recv()

    def grad_hidden_step(j):
        at = chunk(j, TILE)
        g = mul(cot2[...], flat(wd[:, :, at]))
        gg[:, at] = (g * fac_a[:, at]).astype(BF)
        gu[:, at] = (g * fac_b[:, at]).astype(BF)

    loop(ff // TILE, grad_hidden_step)
    swap("mix", part.at[upper], box_mix).wait_send()

    def gam_step(j):
        u = pl.ds(j * 2, 2)
        part[:, chunk(j, TILE)] = times_rows(gg[...], flat(wgu[0, u])) + times_rows(gu[...], flat(wgu[1, u]))

    loop(4, gam_step)
    gam_swap = swap("gam", part.at[upper], box_gam)
    gam_swap.start()
    gam_swap.wait_recv()

    def resid_step(i):
        at = chunk(i, rc)
        g = part[at] + box_gam[at]
        n = normed[at]
        small[1:2] = small[1:2] + jnp.sum(g * n, axis=0, keepdims=True)
        full = cot2[at].astype(F32) + norm_back(g * vecs[1:2], n, scale_mid[at, 0:1])
        box_gam[at] = full
        gmix[at] = full.astype(BF)

    loop(length // rc, resid_step)
    gmix_swap = swap("gmix", gmix.at[lower], gmix.at[upper])
    gmix_swap.start()
    gam_swap.wait_send()

    def ffn_step(j):
        u = pl.ds(j * 2, 2)
        part[:, chunk(j, TILE)] = times_rows(hidden[...], flat(wd[u]))

    loop(4, ffn_step)
    ffn_swap = swap("ffn", part.at[upper], box_ffn)
    ffn_swap.start()
    gmix_swap.wait_recv()
    grad_gated = fac_a.at[:, pl.ds(0, half)]
    grad_gated[...] = times_rows(gmix[...], flat(wout_mine[...]))

    def gconv_step(i):
        for q in (0, 1):
            at = pl.ds(pl.multiple_of(q * length + i * rc, rc), rc)
            window = mixed[q, pl.ds(pl.multiple_of(i * rc, 8), rc + 8)]
            g = grad_gated[at]
            gc = g * c_of(at)
            gconv[q, pl.ds(pl.multiple_of(i * rc, 8), rc)] = gc
            gproj[at, pl.ds(half, half)] = (g * conv[at]).astype(BF)
            for k in range(3):
                spot = (pl.ds(2 + k, 1), pl.ds(pl.multiple_of(c * half, 128), half))
                small[spot] = small[spot] + jnp.sum(gc * window[6 + k : 6 + k + rc], axis=0, keepdims=True)

    loop(length // rc, gconv_step)

    @pl.when(jnp.logical_not(first))
    def _():
        back.start()

    ffn_swap.wait_recv()

    def result_step(i):
        at = chunk(i, rc)
        out_res[at] = (resid[at] + part[at] + box_ffn[at]).astype(BF)

    loop(length // rc, result_step)

    @pl.when(jnp.logical_not(last))
    def _():
        back.wait_recv()

    def gproj_step(i):
        for q in (0, 1):
            at = pl.ds(pl.multiple_of(q * length + i * rc, rc), rc)
            window = gconv[q, pl.ds(pl.multiple_of(i * rc, 8), rc + 8)]
            gm = taps[2] * window[0:rc] + taps[1] * window[1 : rc + 1] + taps[0] * window[2 : rc + 2]
            gproj[at, pl.ds(0, half)] = (gm * x_of(at)).astype(BF)
            gproj[at, pl.ds(2 * half, half)] = (gm * b_of(at)).astype(BF)

    loop(length // rc, gproj_step)
    ffn_swap.wait_send()

    def gai_step(j):
        u = pl.ds(j * 2, 2)
        part[:, chunk(j, TILE)] = times_rows(gproj[...], flat(win[u]))

    loop(4, gai_step)
    gai_swap = swap("gai", part.at[upper], box_gai)
    gai_swap.start()
    swap("gated0", gated_other.at[upper], gated_other.at[upper]).wait_recv()
    swap("gated1", gated_other.at[lower], gated_other.at[lower]).wait_recv()
    stores = [
        (act_in, o_act_in), (act_mid, o_act_mid), (hidden, o_hidden), (gg, o_gg), (gu, o_gu), (gproj, o_proj),
        (gated, o_gated), (gmix, o_mix), (cot2, o_cot), (out_res, result),
    ]
    stores = [pltpu.make_async_copy(a, b, out_sem.at[i]) for i, (a, b) in enumerate(stores)]
    for cp in stores:
        cp.start()
    gai_swap.wait_recv()

    def final_step(i):
        at = chunk(i, rc)
        g = part[at] + box_gai[at]
        n, s = normalize(tok2[at].astype(F32))
        small[0:1] = small[0:1] + jnp.sum(g * n, axis=0, keepdims=True)
        resid[at] = box_gam[at] + norm_back(g * vecs[0:1], n, s)

    loop(length // rc, final_step)
    stores.append(pltpu.make_async_copy(resid, grad_tokens, out_sem.at[10]))
    stores.append(pltpu.make_async_copy(small, o_small, out_sem.at[11]))
    for cp in stores[-2:]:
        cp.start()
    for wait in pending:
        wait()
    act_swap.wait_send()
    gmix_swap.wait_send()
    gai_swap.wait_send()

    @pl.when(jnp.logical_not(last))
    def _():
        fore.wait_send()

    @pl.when(jnp.logical_not(first))
    def _():
        back.wait_send()

    for cp in stores:
        cp.wait()


COPIES = 5 * 12 + 2 * 14


def block_call(tokens, cot, w_in, w_out, w_gate, w_up, w_down, gains, taps):
    length, width = tokens.shape
    rows, ff = w_in.shape[0], w_gate.shape[1] // 2
    half = width // 2
    two = 2 * length
    hbm = pl.BlockSpec(memory_space=pltpu.HBM)
    vm = pl.BlockSpec(memory_space=pltpu.VMEM)

    def out(*shape, dtype=BF):
        return jax.ShapeDtypeStruct(shape, dtype)

    def mem(*shape, dtype=BF):
        return pltpu.VMEM(shape, dtype)

    dma = pltpu.SemaphoreType.DMA
    return pl.pallas_call(
        block_kernel,
        out_shape=(
            out(length, width), out(length, width, dtype=F32), out(two, width), out(two, width), out(two, ff),
            out(two, ff), out(two, ff), out(two, 3 * half), out(two, width), out(two, width), out(two, width),
            out(8, width, dtype=F32),
        ),
        in_specs=[hbm] * 7 + [vm] * 2,
        out_specs=(hbm,) * 12,
        scratch_shapes=[
            mem(8, rows, 3 * half), mem(8, rows, width), mem(2, 8, rows, ff), mem(8, rows, ff), mem(8, 32, 128),
            mem(two, width), mem(two, width), mem(two, width), mem(two, 3 * half, dtype=F32),
            mem(2, length + 8, half, dtype=F32), mem(two, half, dtype=F32), mem(two, width), mem(two, width, dtype=F32),
            mem(length, width, dtype=F32), mem(length, width, dtype=F32), mem(length, width, dtype=F32),
            mem(length, width, dtype=F32), mem(length, width, dtype=F32), mem(length, width, dtype=F32), mem(two, width),
            mem(two, ff), mem(two, ff, dtype=F32), mem(two, ff, dtype=F32), mem(two, ff), mem(two, ff), mem(two, width),
            mem(2, length + 8, half, dtype=F32), mem(two, 3 * half), mem(16, width, dtype=F32), mem(8, width, dtype=F32),
            mem(length, 128, dtype=F32), mem(length, width),
            dma((9,)), dma((COPIES,)), dma((COPIES,)), dma((len(SWAPS),)), dma((len(SWAPS),)), dma((12,)),
        ],
        compiler_params=pltpu.CompilerParams(collective_id=1, has_side_effects=True, vmem_limit_bytes=62 << 20),
    )(tokens, cot, w_in, w_out, w_gate, w_up, w_down, gains, taps)
ORDERS = ("XYZ", "YZX", "ZXY")
SIZES = {"X": (1, 4, 1, 4), "Y": (2, 1, 2, 4), "Z": (2, 4, 2, 1)}


def dims_left(order, phase):
    sizes = [2, 4, 2, 4]
    for axis in order[: phase + 1]:
        for i in {"X": (0, 2), "Y": (1,), "Z": (3,)}[axis]:
            sizes[i] = 1
    return tuple(n for n in sizes if n > 1)


def halves(columns):
    first = columns // 256 * 128
    return (0, first), (first, columns - first)


COUNT = 3
PLACES = 3 * COUNT


def reduce_kernel(*refs):
    n = COUNT
    ins, refs = refs[:10], refs[10:]
    outs, refs = refs[:6], refs[6:]
    held, refs = refs[:n], refs[n:]
    relay, refs = [refs[6 * t : 6 * t + 6] for t in range(n)], refs[6 * n :]
    takes, refs = [refs[6 * t : 6 * t + 6] for t in range(n)], refs[6 * n :]
    bufs, refs = refs[:10], refs[10:]
    turned, refs = refs[:4], refs[4:]
    local_sem, send_sem, recv_sem, spread_send, spread_recv, core_send, core_recv = refs
    o_gate, o_up, o_down, o_in, o_out, o_small = outs
    xl, xh, y, z, c = place()
    x = xh * 2 + xl
    loads = [pltpu.make_async_copy(a, b, local_sem.at[i]) for i, (a, b) in enumerate(zip(ins, bufs))]
    for cp in loads:
        cp.start()
    act_mid, gg, act_in, gproj, small, gu, gated, gmix, cot, hidden = bufs
    mid_t, in_t, gated_t, cot_t = turned
    half = gproj.shape[1] // 3
    ff = gg.shape[1]
    width = half * 2
    quarter = half // 2
    where = {"X": x, "Y": y, "Z": z}
    near = {
        "X": (device(x - 1, y, z, c), device(x + 1, y, z, c)),
        "Y": (device(x, y - 1, z, c), device(x, y + 1, z, c)),
        "Z": (device(x, y, z - 1, c), device(x, y, z + 1, c)),
    }
    replicas = [(dx, dz) for dx in (0, 2) for dz in (1, 3, 2, 0) if dx or dz]
    spread_to = [device(x + dx, y, z + dz, c) for dx, dz in replicas]
    sibling = device(x, y, z, 1 - c)
    far = [device(x + dx, y, z + dz, c) for dx, dz in replicas if (dx, dz) not in ((0, 1), (0, 3))]
    greet([*near["X"], *near["Y"], *near["Z"], *far, sibling])
    pending = []

    def index(order, phase, q):
        at = [slice(None)] * 4
        for a in order[:phase]:
            put(at, a, where[a])
        put(at, order[phase], q)
        return tuple(at)

    def put(at, axis, q):
        if axis == "X":
            at[0], at[2] = q % 2, q // 2
        else:
            at[1 if axis == "Y" else 3] = q

    def key(t, phase, k):
        return (t * 3 + phase) * 6 + k

    def ship(src, dst, to, t, phase, k):
        cp = remote(src, dst, send_sem.at[key(t, phase, k)], recv_sem.at[key(t, phase, k)], to)
        cp.start()
        pending.append(cp)

    def arrived(dst, t, phase, k):
        remote(dst, dst, send_sem.at[key(t, phase, k)], recv_sem.at[key(t, phase, k)], sibling).wait_recv()

    def cols(view, h, t):
        at, size = halves(held[t].shape[-1])[h]
        lead = len(view.shape) - 1
        return view.at[(slice(None),) * lead + (pl.ds(at, size),)]

    def part(ref, t, phase, q, h):
        return cols(ref.at[index(ORDERS[t], phase, q)], h, t)

    def buffers(t, phase):
        ra, rb = relay[t][2 * phase : 2 * phase + 2]
        tl, tr = takes[t][2 * phase : 2 * phase + 2]
        return ra, rb, tl, tr

    def each(dims, body):
        total = 1
        for d in dims:
            total *= d

        def step(i, carry):
            at, rest = [], i
            for d in reversed(dims):
                at.append(rest % d)
                rest = rest // d
            body(tuple(reversed(at)))
            return carry

        if total == 1:
            body(())
        else:
            lax.fori_loop(0, total, step, 0)

    def full(order, phase, q, at):
        idx, k = list(index(order, phase, q)), 0
        for i in range(4):
            if isinstance(idx[i], slice):
                idx[i] = at[k]
                k += 1
        return tuple(idx)

    def begin(t, phase, first=True, second=True):
        order = ORDERS[t]
        p = where[order[phase]]
        left, right = near[order[phase]]
        ra, rb, tl, tr = buffers(t, phase)
        src = held[t]
        far_q, next_q, last_q = (p + 2) % 4, (p + 1) % 4, (p + 3) % 4
        if first:
            ship(part(src, t, phase, far_q, 0), ra, right, t, phase, 0)
            ship(part(src, t, phase, far_q, 1), rb, left, t, phase, 1)
        if second:
            ship(part(src, t, phase, next_q, 1), cols(tl, 1, t), right, t, phase, 2)
            ship(part(src, t, phase, last_q, 0), cols(tr, 0, t), left, t, phase, 3)

    def middle(t, phase):
        order = ORDERS[t]
        p = where[order[phase]]
        left, right = near[order[phase]]
        ra, rb, tl, tr = buffers(t, phase)
        dims = dims_left(order, phase)
        for h, (box, q, to, dst) in enumerate(((ra, (p + 1) % 4, right, tl), (rb, (p + 3) % 4, left, tr))):
            arrived(box, t, phase, h)
            at0, size = halves(held[t].shape[-1])[h]

            def add(at, box=box, q=q, at0=at0, size=size):
                slab = full(order, phase, q, at) + (slice(None), pl.ds(at0, size))
                held[t][slab] = (held[t][slab].astype(F32) + box[at].astype(F32)).astype(BF)

            each(dims, add)
            ship(part(held[t], t, phase, q, h), cols(dst, h, t), to, t, phase, 4 + h)

    def finish(t, phase):
        order = ORDERS[t]
        p = where[order[phase]]
        ra, rb, tl, tr = buffers(t, phase)
        dims = dims_left(order, phase)
        arrived(cols(tl, 1, t), t, phase, 2)
        arrived(cols(tr, 0, t), t, phase, 3)
        arrived(cols(tl, 0, t), t, phase, 4)
        arrived(cols(tr, 1, t), t, phase, 5)

        def add(at):
            slab = full(order, phase, p, at)
            held[t][slab] = (held[t][slab].astype(F32) + tl[at].astype(F32) + tr[at].astype(F32)).astype(BF)

        each(dims, add)

    tile = 256

    def fill(t, step):
        axis = ORDERS[t][0]
        at = [slice(None)] * 4
        put(at, axis, (where[axis] + step) % 4)
        at = tuple(at)
        lead = dims_left(ORDERS[t], 0)

        def block(left, right, start, cols_n, put_at):
            rows = flat(left[at])

            def one(j):
                value = mul(rows, right[:, pl.ds(pl.multiple_of(start + j * tile, 128), tile)]).astype(BF)
                held[t][at + (slice(None), pl.ds(pl.multiple_of(put_at + j * tile, 128), tile))] = value.reshape(
                    lead + (16, tile)
                )

            loop(cols_n // tile, one)

        block((mid_t, mid_t, cot_t)[t], (gg, gu, hidden)[t], 0, ff, 0)
        block(in_t, gproj, t * half, half, ff)
        if t:
            block(gated_t, gmix, c * half + (t - 1) * quarter, quarter, ff + half)

    def turn(source, target):
        size = 128

        def one(i):
            target[:, :, :, :, :, chunk(i, size)] = source[chunk(i, size)].T.reshape(target.shape[:5] + (size,))

        loop(source.shape[0] // size, one)

    for cp in loads[:5]:
        cp.wait()
    tall = jnp.concatenate([small[...], jnp.zeros((120, width), F32)], axis=0)
    held[0][:, :, :, :, :, pl.ds(ff + half, 128)] = tall.T.astype(BF).reshape(2, 4, 2, 4, 16, 128)
    turn(act_mid, mid_t)
    turn(act_in, in_t)
    fill(0, 2)
    begin(0, 0, second=False)
    for cp in loads[5:8]:
        cp.wait()
    turn(gated, gated_t)
    fill(1, 2)
    begin(1, 0, second=False)
    for cp in loads[8:]:
        cp.wait()
    turn(cot, cot_t)
    fill(2, 2)
    begin(2, 0, second=False)
    for t in range(n):
        fill(t, 1)
        fill(t, 3)
        begin(t, 0, first=False)
    for t in range(n):
        fill(t, 0)
    for phase in range(3):
        if phase:
            for t in range(n):
                begin(t, phase)
        for t in range(n):
            middle(t, phase)
        for t in range(n):
            finish(t, phase)
    pieces = (
        ((0, ff, o_gate, c * ff), (ff, half, o_in, c * half), (ff + half, 128, o_small, c * 128)),
        ((0, ff, o_up, c * ff), (ff, half, o_in, width + c * half), (ff + half, quarter, o_out, c * half)),
        ((0, ff, o_down, c * ff), (ff, half, o_in, 2 * width + c * half), (ff + half, quarter, o_out, c * half + quarter)),
    )
    other = (
        ((o_gate, (1 - c) * ff), (o_in, (1 - c) * half), (o_small, (1 - c) * 128)),
        ((o_up, (1 - c) * ff), (o_in, width + (1 - c) * half), (o_out, (1 - c) * half)),
        ((o_down, (1 - c) * ff), (o_in, 2 * width + (1 - c) * half), (o_out, (1 - c) * half + quarter)),
    )
    slot = xh * 4 + z

    def spot(out, row, count, col, size):
        return out.at[pl.ds(pl.multiple_of(row, 16), count), pl.ds(pl.multiple_of(col, 128), size)]

    keeps = []
    for t in range(n):
        for k, (at, size, out, col) in enumerate(pieces[t]):
            piece = held[t].at[xl, y, xh, z, :, pl.ds(at, size)]
            dst = spot(out, slot * 16, 16, col, size)
            for i, to in enumerate(spread_to):
                key_ = (t * 3 + k) * 7 + i
                cp = remote(piece, dst, spread_send.at[key_], spread_recv.at[key_], to)
                cp.start()
                pending.append(cp)
            keeps.append(pltpu.make_async_copy(piece, dst, local_sem.at[t * 3 + k]))
            keeps[-1].start()
    for t in range(n):
        for k, (at, size, out, col) in enumerate(pieces[t]):
            keeps[t * 3 + k].wait()
            for i, (dx, dz) in enumerate(replicas):
                src = ((xh + dx // 2) % 2) * 4 + (z + 4 - dz) % 4
                dst = spot(out, src * 16, 16, col, size)
                key_ = (t * 3 + k) * 7 + i
                remote(dst, dst, spread_send.at[key_], spread_recv.at[key_], sibling).wait_recv()
            whole = spot(out, 0, 128, col, size)
            cp = remote(whole, whole, core_send.at[t * 3 + k], core_recv.at[t * 3 + k], sibling)
            cp.start()
            pending.append(cp)
    for t in range(n):
        for k, (out, col) in enumerate(other[t]):
            dst = spot(out, 0, 128, col, pieces[t][k][1])
            remote(dst, dst, core_send.at[t * 3 + k], core_recv.at[t * 3 + k], sibling).wait_recv()
    for cp in pending:
        cp.wait_send()


def reduce_grads(act_mid, gg, act_in, gproj, small, gu, gated, gmix, cot, hidden):
    n = COUNT
    ins = (act_mid, gg, act_in, gproj, small, gu, gated, gmix, cot, hidden)
    width, ff, two = act_in.shape[1], gg.shape[1], act_in.shape[0]
    half = width // 2
    widths = (ff + half + 128, ff + half + half // 2, ff + half + half // 2)
    lead = (2, 4, 2, 4, 16)
    held = [pltpu.VMEM(lead + (w,), BF) for w in widths]
    relay, takes = [], []
    for t in range(n):
        for phase in range(3):
            dims = dims_left(ORDERS[t], phase)
            for h in (0, 1):
                relay.append(pltpu.VMEM(dims + (16, halves(widths[t])[h][1]), BF))
                takes.append(pltpu.VMEM(dims + (16, widths[t]), BF))
    bufs = [pltpu.VMEM(a.shape, a.dtype) for a in ins]
    turned = [pltpu.VMEM(lead + (two,), BF)] * 4
    dma = pltpu.SemaphoreType.DMA
    hbm = pl.BlockSpec(memory_space=pltpu.HBM)
    rows = 128
    outs = (2 * ff, 2 * ff, 2 * ff, 3 * width, width, 256)
    return pl.pallas_call(
        reduce_kernel,
        out_shape=tuple(jax.ShapeDtypeStruct((rows, w), BF) for w in outs),
        in_specs=[hbm] * len(ins),
        out_specs=(hbm,) * len(outs),
        scratch_shapes=held + relay + takes + bufs + turned
        + [dma((10,)), dma((54,)), dma((54,)), dma((63,)), dma((63,)), dma((9,)), dma((9,))],
        compiler_params=pltpu.CompilerParams(collective_id=2, has_side_effects=True, vmem_limit_bytes=62 << 20),
    )(*ins)


def local(tokens, norm_in, w_in, conv_w, w_out, norm_mid, w_gate, w_up, w_down, cotangent):
    gains = jnp.stack([norm_in, norm_mid])
    (
        result, grad_tokens, act_in, act_mid, hidden, gg, gu, gproj, gated, gmix, cot, small
    ) = block_call(tokens[0], cotangent[0], w_in, w_out, w_gate, w_up, w_down, gains, conv_w.T)
    sums = reduce_grads(act_mid, gg, act_in, gproj, small, gu, gated, gmix, cot, hidden)
    g_gate, g_up, g_down, g_in, g_out, g_small = (s.astype(F32) for s in sums)
    g_small = g_small[:, :128] + g_small[:, 128:]
    return (
        result[None],
        grad_tokens[None],
        g_small[:, 0],
        g_in,
        g_small[:, 2:5],
        g_out,
        g_small[:, 1],
        g_gate,
        g_up,
        g_down,
    )


def solution(mesh):
    row, act, vec = P("shard", None), P("replica", "shard", None), P("shard")
    in_specs = (act, vec, row, row, row, vec, row, row, row, act)
    out_specs = (act, act, vec, row, row, row, vec, row, row, row)
    return jax.shard_map(local, mesh=mesh, in_specs=in_specs, out_specs=out_specs, check_vma=False)
```

profile of v0, /device:TPU:27, one launch (start us, length us, event | category | flops | bytes accessed | tf_op | source)
XLA Modules:
  0.0 314.4 jit_solution(15159562948127503315)
XLA Ops:
  0.6 1.2 pad_maximum_fusion.gains
  1.8 161.6 %shard_map.177 = (bf16[256,1024]{1,0:T(8,128)(2,1)}, f32[256,1024]{1,0:T(8,128)}, bf16[512,1024]{1,0:T(8,128)(2,1)}, bf16[512,1024]{1,0:T(8,128)(2,1)}, bf16[512...) custom-call(bf16[256,1024]{1,0:T(8,128)(2,1)} %bitcast.8, ...), custom_call_target="tpu_custom_call" | custom-call | tf_op jit(solution)/shard_map/pallas_call | solution.py:498
  163.4 138.6 %shard_map.178 = (bf16[128,4608]{1,0:T(8,128)(2,1)}, bf16[128,4608]{1,0:T(8,128)(2,1)}, bf16[128,4608]{1,0:T(8,128)(2,1)}, bf16[128,3072]{1,0:T(8,128)(2,1)}, bf...) custom-call(bf16[512,1024]{1,0:T(8,128)(2,1)} %get-tuple-element.30.refs_0_, ...), custom_call_target="tpu_custom_call" | custom-call | tf_op jit(solution)/shard_map/pallas_call | solution.py:819
  302.1 0.0 copy-start.4
  302.1 0.9 convert_element_type.18
  303.0 0.7 slice_reduce_fusion
  303.7 0.1 slice.23
  303.8 0.7 copy.21
  304.4 0.0 copy-start.2
  304.4 1.9 convert_element_type.20
  306.3 0.0 copy-done.4
  306.3 1.3 convert_element_type.19
  307.6 0.0 copy-done.2
  307.6 0.0 copy-start.1
  307.6 1.6 convert_element_type.21
  309.3 0.0 copy-done.1
  309.3 0.0 copy-start
  309.3 1.6 convert_element_type.22
  310.9 0.0 copy-done
  310.9 0.0 copy-start.5
  310.9 0.0 copy-start.3
  310.9 1.6 convert_element_type.23
  312.6 0.0 copy-done.5
  312.6 0.8 copy.24
  313.4 0.0 copy-done.3
  313.4 1.0 copy.25
  (1 shorter events, 0.0 us)
Async XLA Ops:
  302.1 4.3 %copy-start.4 = (bf16[128,3072]{1,0:T(8,128)(2,1)S(1)}, bf16[128,3072]{1,0:T(8,128)(2,1)}, u32[]{:S(2)}) copy-start(bf16[128,3072]{1,0:T(8,128)(2,1)} %get-tuple-element.41) | copy-start | bytes 2359300
  304.4 3.2 %copy-start.2 = (bf16[128,4608]{1,0:T(8,128)(2,1)S(1)}, bf16[128,4608]{1,0:T(8,128)(2,1)}, u32[]{:S(2)}) copy-start(bf16[128,4608]{1,0:T(8,128)(2,1)} %get-tuple-element.43) | copy-start | bytes 3538948
  307.6 1.6 copy-start.1
  309.3 1.6 copy-start
  310.9 1.6 copy-start.5
  310.9 2.4 copy-start.3
where the time goes:
time: 315 us; the launch traced here: 314 us
  Pallas kernels  300 us (95%)
  other arithmetic  10.2 us (3%)
  local copies, waits for them, and re-layouts  3.22 us (1%)
    pallas_call x1, Pallas kernels, block_call(): pl.pallas_call(block_kernel, out_shape=(out(length, width), out(length, w...  162 us
    pallas_call x1, Pallas kernels, reduce_grads(): pl.pallas_call(reduce_kernel, out_shape=tuple((jax.ShapeDtypeStruct((rows...  139 us
    convert_element_type x6, other arithmetic, local(): g_gate, g_up, g_down, g_in, g_out, g_small = (s.astype(F32) for s in sums)  9.03 us

commit v1 on v0

--- a/solution.py
+++ b/solution.py
@@ -70,16 +70,62 @@
     return value.reshape(-1, value.shape[-1])
 
 
+ORDERS = ("XYZ", "YZX", "ZXY") * 2
+SIZES = {"X": (1, 4, 1, 4), "Y": (2, 1, 2, 4), "Z": (2, 4, 2, 1)}
+
+
+def dims_left(order, phase):
+    sizes = [2, 4, 2, 4]
+    for axis in order[: phase + 1]:
+        for i in {"X": (0, 2), "Y": (1,), "Z": (3,)}[axis]:
+            sizes[i] = 1
+    return tuple(n for n in sizes if n > 1)
+
+
+def halves(columns):
+    first = columns // 256 * 128
+    return (0, first), (first, columns - first)
+
+
+EARLY = 1536
+WIDE = 768
+LEAD = (2, 4, 2, 4, 16)
+
+
+def put(at, axis, q):
+    if axis == "X":
+        at[0], at[2] = q % 2, q // 2
+    else:
+        at[1 if axis == "Y" else 3] = q
+
+
+def quarter_at(axis, q):
+    at = [slice(None)] * 4
+    put(at, axis, q)
+    return tuple(at)
+
+
+def turn(source, target):
+    size = 128
+
+    def one(i):
+        target[:, :, :, :, :, chunk(i, size)] = source[chunk(i, size)].T.reshape(LEAD + (size,))
+
+    loop(source.shape[0] // size, one)
+
+
 SWAPS = ("tokens", "cot", "gated0", "gated1", "mix", "act", "ffn", "gam", "gmix", "gai", "fore", "back")
 TILE = 256
 
 
 def block_kernel(
     tokens, cot, w_in, w_out, w_gate, w_up, w_down, gains, taps_in,
-    result, grad_tokens, o_act_in, o_act_mid, o_hidden, o_gg, o_gu, o_proj, o_gated, o_mix, o_cot, o_small,
+    result, grad_tokens, o_in_t, o_mid_t, o_hidden, o_gg, o_gu, o_proj, o_gated, o_mix, o_cot_t, o_small,
+    own0, left0, right0, own1, left1, right1, own2, left2, right2,
     win, wout, wgu, wd, ext, tok2, cot2, act_in, proj, mixed, conv, gated, part, box_mix, box_ffn, box_gam, box_gai,
-    resid, normed, act_mid, hidden, fac_a, fac_b, gg, gu, gmix, gconv, gproj, vecs, small, scale_mid, out_res,
-    local_sem, send_sem, recv_sem, core_send, core_recv, out_sem,
+    resid, normed, act_mid, hidden, held, gg, gu, gmix, gconv, gproj, vecs, small, scale_mid, out_res, mid_t, cot_t,
+    far_a0, far_b0, far_a1, far_b1, far_a2, far_b2,
+    local_sem, send_sem, recv_sem, core_send, core_recv, out_sem, early_send, early_recv,
 ):
     xl, xh, y, z, c = place()
     x = xh * 2 + xl
@@ -112,7 +158,12 @@
         cp.start()
     greet([xp, xm, yp, ym, zp, zm, sibling, nxt, prv])
 
-    pending = []
+    pending, stores, used = [], [], []
+
+    def store(src, dst):
+        stores.append(pltpu.make_async_copy(src, dst, out_sem.at[len(used)]))
+        used.append(dst)
+        stores[-1].start()
 
     def fire(cp):
         cp.start()
@@ -123,7 +174,7 @@
         return remote(src, dst, core_send.at[k], core_recv.at[k], sibling if to is None else to)
 
     def wd_part(g, u):
-        return wd.at[u, pl.ds(pl.multiple_of(g * (rows // 2), rows // 2), rows // 2)]
+        return wd.at[u, pl.ds(pl.multiple_of(g * (rows // 4), rows // 4), rows // 4)]
 
     parts = [
         (lambda g, u: ext.at[u], False),
@@ -131,6 +182,7 @@
         (lambda g, u: wgu.at[g, u], True),
         (lambda g, u: wout.at[u], False),
         (wd_part, True),
+        (lambda g, u: wd.at[u, pl.ds(rows // 2, rows // 2)], False),
     ]
     keys, count = {}, 0
     for p in range(len(parts)):
@@ -171,10 +223,12 @@
             u = over(dy) if other else at_y(dy)
             send(cut(parts[p][0](mine, u), h), (zp, zm)[h], keys[p, ("z", other, dy, h)])
 
-    def launch(p):
+    def launch_y(p):
         view = parts[p][0]
         send(view(mine, own), yp, keys[p, "y+"])
         send(view(mine, own), ym, keys[p, "y-"])
+
+    def launch_x(p):
         for h in (0, 1):
             send_x(p, 0, h)
 
@@ -198,9 +252,9 @@
             send_z(p, 0, 2, h)
             send_x(p, 2, h)
 
-    def stage_c(p, dys=(0, -1, 1, 2)):
+    def stage_c(p, *dys):
         view = parts[p][0]
-        for dy in dys:
+        for dy in dys or (0, -1, 1, 2):
             for h in (0, 1):
                 got(cut(view(mine, over(dy)), h), keys[p, ("x", dy, h)])
                 send_z(p, 1, dy, h)
@@ -213,23 +267,27 @@
                     got(cut(view(1 - mine, at_y(dy)), h), keys[p, ("z", 0, dy, h)])
                 got(cut(view(1 - mine, over(dy)), h), keys[p, ("z", 1, dy, h)])
 
-    EXT, WIN, WGU, WOUT, WD = range(5)
+    EXT, WIN, WGU, WOUT, WDZ, WDX = range(6)
     lower, upper = pl.ds(0, length), pl.ds(length, length)
-    launch(EXT)
+    launch_y(EXT)
+    launch_x(EXT)
+    for cp in loads[3:5]:
+        cp.wait()
+    launch_y(WGU)
+    launch_x(WGU)
     for cp in loads[:3]:
         cp.wait()
-    launch(WIN)
-    for cp in loads[3:5]:
-        cp.wait()
-    launch(WGU)
+    launch_y(WIN)
+    launch_x(WIN)
     for cp in loads[7:]:
         cp.wait()
     fire(swap("tokens", tok2.at[lower], tok2.at[upper]))
     fire(swap("cot", cot2.at[lower], cot2.at[upper]))
     for cp in loads[5:7]:
         cp.wait()
-    launch(WOUT)
-    launch(WD)
+    launch_x(WOUT)
+    launch_x(WDZ)
+    launch_x(WDX)
     for stage in (stage_a, stage_b, stage_c):
         stage(EXT)
     for u in range(8):
@@ -237,7 +295,6 @@
     small[...] = jnp.zeros_like(small)
     mixed[:, pl.ds(0, 8)] = jnp.zeros((2, 8, half), F32)
     gconv[:, pl.ds(length, 8)] = jnp.zeros((2, 8, half), F32)
-    stage_a(WIN)
     swap("tokens", tok2.at[lower], tok2.at[upper]).wait_recv()
     rc = 32
 
@@ -246,8 +303,24 @@
         act_in[chunk(i, rc)] = (v * vecs[0:1]).astype(BF)
 
     loop(2 * length // rc, norm_in_step)
+    turn(act_in, mid_t)
+    store(mid_t, o_in_t)
+    in_store = stores.pop()
+    stage_c(WGU, 0)
+    stage_a(WGU)
+    launch_y(WOUT)
+    stage_a(WIN)
+    launch_y(WDZ)
+    stage_c(WGU, -1, 1)
+    stage_b(WGU)
+    stage_a(WOUT)
+    launch_y(WDX)
     stage_b(WIN)
-    stage_a(WGU)
+    stage_c(WGU, 2)
+    stage_a(WDZ)
+    swap("cot", cot2.at[lower], cot2.at[upper]).wait_recv()
+    turn(cot2, cot_t)
+    store(cot_t, o_cot_t)
     stage_c(WIN)
 
     def proj_step(j):
@@ -277,7 +350,9 @@
     def _():
         fore.start()
 
-    stage_b(WGU)
+    stage_b(WOUT)
+    stage_c(WDZ, 0)
+    stage_a(WDX)
 
     @pl.when(jnp.logical_not(first))
     def _():
@@ -299,8 +374,9 @@
     gated_other = gated.at[:, pl.ds(pl.multiple_of((1 - c) * half, 128), half)]
     fire(swap("gated0", gated_mine.at[lower], gated_mine.at[upper]))
     fire(swap("gated1", gated_mine.at[upper], gated_mine.at[lower]))
-    for stage in (stage_a, stage_b, stage_c):
-        stage(WOUT)
+    stage_b(WDZ)
+    stage_c(WDZ, -1, 1)
+    stage_c(WOUT)
     wout_mine = wout.at[pl.ds(pl.multiple_of(c * 4, 4), 4)]
 
     def mix_step(j):
@@ -309,7 +385,7 @@
     loop(width // TILE, mix_step)
     mix_swap = swap("mix", part.at[upper], box_mix)
     mix_swap.start()
-    stage_c(WGU, (0, -1))
+    stage_b(WDX)
     mix_swap.wait_recv()
 
     def norm_mid_step(i):
@@ -324,12 +400,45 @@
     loop(length // rc, norm_mid_step)
     act_swap = swap("act", act_mid.at[lower], act_mid.at[upper])
     act_swap.start()
-    stage_c(WGU, (1, 2))
-    stage_a(WD)
+    stage_c(WDZ, 2)
     act_swap.wait_recv()
-    stage_b(WD)
-    stage_c(WD)
+    in_store.wait()
+    turn(act_mid, mid_t)
+    store(mid_t, o_mid_t)
     stage_d(WGU)
+
+    where = {"X": x, "Y": y, "Z": z}
+    near = {"X": (xm, xp), "Y": (ym, yp), "Z": (zm, zp)}
+    landings = ((own0, left0, right0), (own1, left1, right1), (own2, left2, right2))
+    relays = ((far_a0, far_b0), (far_a1, far_b1), (far_a2, far_b2))
+    eh = EARLY // 2
+
+    def early_at(t, step):
+        axis = ORDERS[t][0]
+        return quarter_at(axis, (where[axis] + step) % 4)
+
+    def early_fill(t, step):
+        at = early_at(t, step)
+        lead = dims_left(ORDERS[t], 0) + (16, WIDE)
+        tall, right = flat((mid_t, mid_t, cot_t)[t][at]), (gg, gu, hidden)[t]
+
+        def one(j):
+            value = mul(tall, right[:, chunk(j, WIDE)]).astype(BF)
+            held[(t,) + at + (slice(None), chunk(j, WIDE))] = value.reshape(lead)
+
+        loop(EARLY // WIDE, one)
+
+    def early_cols(view, h):
+        return view.at[(slice(None),) * (len(view.shape) - 1) + (pl.ds(h * eh, eh),)]
+
+    def early_copy(t, k):
+        to_right = k in (0, 2, 4)
+        h = (0, 1, 1, 0, 0, 1)[k]
+        step = 2 if k < 2 else (1 if to_right else 3)
+        src = early_cols(held.at[(t,) + early_at(t, step)], h)
+        dst = relays[t][k] if k < 2 else early_cols(landings[t][1 if to_right else 2], h)
+        to = near[ORDERS[t][0]][1 if to_right else 0]
+        return remote(src, dst, early_send.at[t * 6 + k], early_recv.at[t * 6 + k], to)
 
     def gate_step(j):
         at = chunk(j, TILE)
@@ -338,20 +447,42 @@
         sig = jax.nn.sigmoid(gate)
         silu = gate * sig
         hidden[:, at] = (silu * up).astype(BF)
-        fac_b[:, at] = silu
-        fac_a[:, at] = up * (sig * (1.0 + gate * (1.0 - sig)))
+        factor = up * (sig * (1.0 + gate * (1.0 - sig)))
+        spot = (slice(None),) * 4 + (chunk(j % 6, TILE),)
+        held[(j // 6, 0) + spot] = factor.astype(BF).reshape(LEAD[1:] + (TILE,))
+        held[(j // 6, 1) + spot] = silu.astype(BF).reshape(LEAD[1:] + (TILE,))
 
     loop(ff // TILE, gate_step)
-    stage_d(WD)
-    swap("cot", cot2.at[lower], cot2.at[upper]).wait_recv()
+    store(hidden, o_hidden)
+    early_fill(2, 2)
+    fire(early_copy(2, 0))
+    fire(early_copy(2, 1))
+    early_fill(2, 1)
+    fire(early_copy(2, 2))
+    early_fill(2, 3)
+    fire(early_copy(2, 3))
+    early_fill(2, 0)
+    store(held.at[(2,) + early_at(2, 0)], landings[2][0])
+    stage_c(WDX)
+    stage_d(WDZ)
 
     def grad_hidden_step(j):
         at = chunk(j, TILE)
         g = mul(cot2[...], flat(wd[:, :, at]))
-        gg[:, at] = (g * fac_a[:, at]).astype(BF)
-        gu[:, at] = (g * fac_b[:, at]).astype(BF)
+        spot = (slice(None),) * 4 + (chunk(j % 6, TILE),)
+        gg[:, at] = (g * flat(held[(j // 6, 0) + spot]).astype(F32)).astype(BF)
+        gu[:, at] = (g * flat(held[(j // 6, 1) + spot]).astype(F32)).astype(BF)
 
     loop(ff // TILE, grad_hidden_step)
+    store(gg, o_gg)
+    store(gu, o_gu)
+    for t in (0, 1):
+        early_fill(t, 2)
+        fire(early_copy(t, 0))
+        fire(early_copy(t, 1))
+    for t in (0, 1):
+        early_fill(t, 1)
+        fire(early_copy(t, 2))
     swap("mix", part.at[upper], box_mix).wait_send()
 
     def gam_step(j):
@@ -361,6 +492,9 @@
     loop(4, gam_step)
     gam_swap = swap("gam", part.at[upper], box_gam)
     gam_swap.start()
+    for t in (0, 1):
+        early_fill(t, 3)
+        fire(early_copy(t, 3))
     gam_swap.wait_recv()
 
     def resid_step(i):
@@ -375,6 +509,9 @@
     loop(length // rc, resid_step)
     gmix_swap = swap("gmix", gmix.at[lower], gmix.at[upper])
     gmix_swap.start()
+    for t in (0, 1):
+        early_fill(t, 0)
+        store(held.at[(t,) + early_at(t, 0)], landings[t][0])
     gam_swap.wait_send()
 
     def ffn_step(j):
@@ -382,17 +519,44 @@
         part[:, chunk(j, TILE)] = times_rows(hidden[...], flat(wd[u]))
 
     loop(4, ffn_step)
+    for t in range(3):
+        for k in (0, 1):
+            early_copy(t, k).wait_recv()
+            at = early_at(t, (1, 3)[k])
+            box = relays[t][k]
+            dims = dims_left(ORDERS[t], 0)
+            total = dims[0] * dims[1] * (dims[2] if len(dims) > 2 else 1)
+
+            def add(i, at=at, box=box, dims=dims, t=t, k=k):
+                places, rest = [], i
+                for d in reversed(dims):
+                    places.append(rest % d)
+                    rest = rest // d
+                places = tuple(reversed(places))
+                left_over = iter(places)
+                spot = (t,) + tuple(next(left_over) if isinstance(a, slice) else a for a in at)
+                spot = spot + (slice(None), pl.ds(k * eh, eh))
+                held[spot] = (held[spot].astype(F32) + box[places].astype(F32)).astype(BF)
+
+            loop(total, add)
+            fire(early_copy(t, 4 + k))
     ffn_swap = swap("ffn", part.at[upper], box_ffn)
     ffn_swap.start()
+
+    def own_ffn_step(i):
+        at = chunk(i, rc)
+        resid[at] = resid[at] + part[at]
+
+    loop(length // rc, own_ffn_step)
     gmix_swap.wait_recv()
-    grad_gated = fac_a.at[:, pl.ds(0, half)]
-    grad_gated[...] = times_rows(gmix[...], flat(wout_mine[...]))
+    for q in (0, 1):
+        box_mix[:, pl.ds(q * half, half)] = times_rows(gmix[pl.ds(q * length, length)], flat(wout_mine[...]))
 
     def gconv_step(i):
         for q in (0, 1):
             at = pl.ds(pl.multiple_of(q * length + i * rc, rc), rc)
             window = mixed[q, pl.ds(pl.multiple_of(i * rc, 8), rc + 8)]
-            g = grad_gated[at]
+            g = box_mix[pl.ds(pl.multiple_of(i * rc, rc), rc), pl.ds(q * half, half)]
             gc = g * c_of(at)
             gconv[q, pl.ds(pl.multiple_of(i * rc, 8), rc)] = gc
             gproj[at, pl.ds(half, half)] = (g * conv[at]).astype(BF)
@@ -405,14 +569,6 @@
     @pl.when(jnp.logical_not(first))
     def _():
         back.start()
-
-    ffn_swap.wait_recv()
-
-    def result_step(i):
-        at = chunk(i, rc)
-        out_res[at] = (resid[at] + part[at] + box_ffn[at]).astype(BF)
-
-    loop(length // rc, result_step)
 
     @pl.when(jnp.logical_not(last))
     def _():
@@ -436,15 +592,19 @@
     loop(4, gai_step)
     gai_swap = swap("gai", part.at[upper], box_gai)
     gai_swap.start()
+    ffn_swap.wait_recv()
+
+    def result_step(i):
+        at = chunk(i, rc)
+        out_res[at] = (resid[at] + box_ffn[at]).astype(BF)
+
+    loop(length // rc, result_step)
     swap("gated0", gated_other.at[upper], gated_other.at[upper]).wait_recv()
     swap("gated1", gated_other.at[lower], gated_other.at[lower]).wait_recv()
-    stores = [
-        (act_in, o_act_in), (act_mid, o_act_mid), (hidden, o_hidden), (gg, o_gg), (gu, o_gu), (gproj, o_proj),
-        (gated, o_gated), (gmix, o_mix), (cot2, o_cot), (out_res, result),
-    ]
-    stores = [pltpu.make_async_copy(a, b, out_sem.at[i]) for i, (a, b) in enumerate(stores)]
-    for cp in stores:
-        cp.start()
+    store(gproj, o_proj)
+    store(gated, o_gated)
+    store(gmix, o_mix)
+    store(out_res, result)
     gai_swap.wait_recv()
 
     def final_step(i):
@@ -455,10 +615,11 @@
         resid[at] = box_gam[at] + norm_back(g * vecs[0:1], n, s)
 
     loop(length // rc, final_step)
-    stores.append(pltpu.make_async_copy(resid, grad_tokens, out_sem.at[10]))
-    stores.append(pltpu.make_async_copy(small, o_small, out_sem.at[11]))
-    for cp in stores[-2:]:
-        cp.start()
+    store(resid, grad_tokens)
+    store(small, o_small)
+    for t in range(3):
+        for k in (2, 3, 4, 5):
+            early_copy(t, k).wait_recv()
     for wait in pending:
         wait()
     act_swap.wait_send()
@@ -477,7 +638,7 @@
         cp.wait()
 
 
-COPIES = 5 * 12 + 2 * 14
+COPIES = 6 * 12 + 2 * 14
 
 
 def block_call(tokens, cot, w_in, w_out, w_gate, w_up, w_down, gains, taps):
@@ -494,68 +655,52 @@
     def mem(*shape, dtype=BF):
         return pltpu.VMEM(shape, dtype)
 
+    firsts = [dims_left(ORDERS[t], 0) + (16,) for t in range(3)]
+    early = [out(*firsts[t], EARLY) for t in range(3) for _ in range(3)]
+    relays = [mem(*firsts[t], EARLY // 2) for t in range(3) for _ in range(2)]
     dma = pltpu.SemaphoreType.DMA
     return pl.pallas_call(
         block_kernel,
         out_shape=(
-            out(length, width), out(length, width, dtype=F32), out(two, width), out(two, width), out(two, ff),
-            out(two, ff), out(two, ff), out(two, 3 * half), out(two, width), out(two, width), out(two, width),
-            out(8, width, dtype=F32),
+            out(length, width), out(length, width, dtype=F32), out(*LEAD, two), out(*LEAD, two), out(two, ff),
+            out(two, ff), out(two, ff), out(two, 3 * half), out(two, width), out(two, width), out(*LEAD, two),
+            out(8, width, dtype=F32), *early,
         ),
         in_specs=[hbm] * 7 + [vm] * 2,
-        out_specs=(hbm,) * 12,
+        out_specs=(hbm,) * 21,
         scratch_shapes=[
             mem(8, rows, 3 * half), mem(8, rows, width), mem(2, 8, rows, ff), mem(8, rows, ff), mem(8, 32, 128),
             mem(two, width), mem(two, width), mem(two, width), mem(two, 3 * half, dtype=F32),
             mem(2, length + 8, half, dtype=F32), mem(two, half, dtype=F32), mem(two, width), mem(two, width, dtype=F32),
             mem(length, width, dtype=F32), mem(length, width, dtype=F32), mem(length, width, dtype=F32),
             mem(length, width, dtype=F32), mem(length, width, dtype=F32), mem(length, width, dtype=F32), mem(two, width),
-            mem(two, ff), mem(two, ff, dtype=F32), mem(two, ff, dtype=F32), mem(two, ff), mem(two, ff), mem(two, width),
+            mem(two, ff), mem(3, *LEAD, EARLY), mem(two, ff), mem(two, ff), mem(two, width),
             mem(2, length + 8, half, dtype=F32), mem(two, 3 * half), mem(16, width, dtype=F32), mem(8, width, dtype=F32),
-            mem(length, 128, dtype=F32), mem(length, width),
-            dma((9,)), dma((COPIES,)), dma((COPIES,)), dma((len(SWAPS),)), dma((len(SWAPS),)), dma((12,)),
+            mem(length, 128, dtype=F32), mem(length, width), mem(*LEAD, two), mem(*LEAD, two), *relays,
+            dma((9,)), dma((COPIES,)), dma((COPIES,)), dma((len(SWAPS),)), dma((len(SWAPS),)), dma((15,)), dma((18,)), dma((18,)),
         ],
         compiler_params=pltpu.CompilerParams(collective_id=1, has_side_effects=True, vmem_limit_bytes=62 << 20),
     )(tokens, cot, w_in, w_out, w_gate, w_up, w_down, gains, taps)
-ORDERS = ("XYZ", "YZX", "ZXY")
-SIZES = {"X": (1, 4, 1, 4), "Y": (2, 1, 2, 4), "Z": (2, 4, 2, 1)}
-
-
-def dims_left(order, phase):
-    sizes = [2, 4, 2, 4]
-    for axis in order[: phase + 1]:
-        for i in {"X": (0, 2), "Y": (1,), "Z": (3,)}[axis]:
-            sizes[i] = 1
-    return tuple(n for n in sizes if n > 1)
-
-
-def halves(columns):
-    first = columns // 256 * 128
-    return (0, first), (first, columns - first)
-
-
-COUNT = 3
-PLACES = 3 * COUNT
+COUNT = 6
 
 
 def reduce_kernel(*refs):
     n = COUNT
     ins, refs = refs[:10], refs[10:]
+    begun, refs = refs[:9], refs[9:]
     outs, refs = refs[:6], refs[6:]
     held, refs = refs[:n], refs[n:]
     relay, refs = [refs[6 * t : 6 * t + 6] for t in range(n)], refs[6 * n :]
     takes, refs = [refs[6 * t : 6 * t + 6] for t in range(n)], refs[6 * n :]
     bufs, refs = refs[:10], refs[10:]
-    turned, refs = refs[:4], refs[4:]
+    turned, refs = refs[:1], refs[1:]
     local_sem, send_sem, recv_sem, spread_send, spread_recv, core_send, core_recv = refs
     o_gate, o_up, o_down, o_in, o_out, o_small = outs
     xl, xh, y, z, c = place()
     x = xh * 2 + xl
     loads = [pltpu.make_async_copy(a, b, local_sem.at[i]) for i, (a, b) in enumerate(zip(ins, bufs))]
-    for cp in loads:
-        cp.start()
-    act_mid, gg, act_in, gproj, small, gu, gated, gmix, cot, hidden = bufs
-    mid_t, in_t, gated_t, cot_t = turned
+    mid_t, gg, in_t, gproj, small, gu, gated, gmix, cot_t, hidden = bufs
+    (gated_t,) = turned
     half = gproj.shape[1] // 3
     ff = gg.shape[1]
     width = half * 2
@@ -566,11 +711,16 @@
         "Y": (device(x, y - 1, z, c), device(x, y + 1, z, c)),
         "Z": (device(x, y, z - 1, c), device(x, y, z + 1, c)),
     }
-    replicas = [(dx, dz) for dx in (0, 2) for dz in (1, 3, 2, 0) if dx or dz]
-    spread_to = [device(x + dx, y, z + dz, c) for dx, dz in replicas]
+    taken = []
+    for t in range(3):
+        at = quarter_at(ORDERS[t][0], where[ORDERS[t][0]])
+        boxes = (held[t].at[at], takes[t][0], takes[t][1])
+        taken += [pltpu.make_async_copy(begun[3 * t + k], boxes[k], local_sem.at[10 + 3 * t + k]) for k in range(3)]
+    for cp in (*loads, *taken):
+        cp.start()
+    across, beyond = device(x + 2, y, z, c), device(x, y, z + 2, c)
     sibling = device(x, y, z, 1 - c)
-    far = [device(x + dx, y, z + dz, c) for dx, dz in replicas if (dx, dz) not in ((0, 1), (0, 3))]
-    greet([*near["X"], *near["Y"], *near["Z"], *far, sibling])
+    greet([*near["X"], *near["Y"], *near["Z"], across, beyond, sibling])
     pending = []
 
     def index(order, phase, q):
@@ -579,12 +729,6 @@
             put(at, a, where[a])
         put(at, order[phase], q)
         return tuple(at)
-
-    def put(at, axis, q):
-        if axis == "X":
-            at[0], at[2] = q % 2, q // 2
-        else:
-            at[1 if axis == "Y" else 3] = q
 
     def key(t, phase, k):
         return (t * 3 + phase) * 6 + k
@@ -672,18 +816,20 @@
         p = where[order[phase]]
         ra, rb, tl, tr = buffers(t, phase)
         dims = dims_left(order, phase)
-        arrived(cols(tl, 1, t), t, phase, 2)
-        arrived(cols(tr, 0, t), t, phase, 3)
-        arrived(cols(tl, 0, t), t, phase, 4)
-        arrived(cols(tr, 1, t), t, phase, 5)
+        if t < 3 and phase == 0:
+            for cp in taken[3 * t : 3 * t + 3]:
+                cp.wait()
+        else:
+            arrived(cols(tl, 1, t), t, phase, 2)
+            arrived(cols(tr, 0, t), t, phase, 3)
+            arrived(cols(tl, 0, t), t, phase, 4)
+            arrived(cols(tr, 1, t), t, phase, 5)
 
         def add(at):
             slab = full(order, phase, p, at)
             held[t][slab] = (held[t][slab].astype(F32) + tl[at].astype(F32) + tr[at].astype(F32)).astype(BF)
 
         each(dims, add)
-
-    tile = 256
 
     def fill(t, step):
         axis = ORDERS[t][0]
@@ -695,112 +841,150 @@
         def block(left, right, start, cols_n, put_at):
             rows = flat(left[at])
 
-            def one(j):
-                value = mul(rows, right[:, pl.ds(pl.multiple_of(start + j * tile, 128), tile)]).astype(BF)
-                held[t][at + (slice(None), pl.ds(pl.multiple_of(put_at + j * tile, 128), tile))] = value.reshape(
-                    lead + (16, tile)
-                )
-
-            loop(cols_n // tile, one)
-
-        block((mid_t, mid_t, cot_t)[t], (gg, gu, hidden)[t], 0, ff, 0)
-        block(in_t, gproj, t * half, half, ff)
-        if t:
-            block(gated_t, gmix, c * half + (t - 1) * quarter, quarter, ff + half)
-
-    def turn(source, target):
-        size = 128
-
-        def one(i):
-            target[:, :, :, :, :, chunk(i, size)] = source[chunk(i, size)].T.reshape(target.shape[:5] + (size,))
-
-        loop(source.shape[0] // size, one)
+            value = mul(rows, right[:, pl.ds(pl.multiple_of(start, 128), cols_n)]).astype(BF)
+            held[t][at + (slice(None), pl.ds(put_at, cols_n))] = value.reshape(lead + (16, cols_n))
+
+        i = t % 3
+        left, right = (mid_t, mid_t, cot_t)[i], (gg, gu, hidden)[i]
+        block(left, right, EARLY, ff - EARLY, 0)
+        block(in_t, gproj, i * half, half, ff - EARLY)
+        if i:
+            block(gated_t, gmix, c * half + (i - 1) * quarter, quarter, ff - EARLY + half)
 
     for cp in loads[:5]:
         cp.wait()
     tall = jnp.concatenate([small[...], jnp.zeros((120, width), F32)], axis=0)
-    held[0][:, :, :, :, :, pl.ds(ff + half, 128)] = tall.T.astype(BF).reshape(2, 4, 2, 4, 16, 128)
-    turn(act_mid, mid_t)
-    turn(act_in, in_t)
-    fill(0, 2)
-    begin(0, 0, second=False)
-    for cp in loads[5:8]:
+    held[3][:, :, :, :, :, pl.ds(ff - EARLY + half, 128)] = tall.T.astype(BF).reshape(2, 4, 2, 4, 16, 128)
+    fill(3, 2)
+    begin(3, 0, second=False)
+    for cp in loads[5:]:
         cp.wait()
     turn(gated, gated_t)
-    fill(1, 2)
-    begin(1, 0, second=False)
-    for cp in loads[8:]:
-        cp.wait()
-    turn(cot, cot_t)
-    fill(2, 2)
-    begin(2, 0, second=False)
-    for t in range(n):
+    for t in (4, 5):
+        fill(t, 2)
+        begin(t, 0, second=False)
+    for t in (0, 1, 2):
+        finish(t, 0)
+        begin(t, 1)
+    for t in (3, 4, 5):
         fill(t, 1)
         fill(t, 3)
         begin(t, 0, first=False)
+    for t in (0, 1, 2):
+        middle(t, 1)
+    for t in (3, 4, 5):
+        middle(t, 0)
+    for t in (3, 4, 5):
+        fill(t, 0)
+    for t in (3, 4, 5):
+        finish(t, 0)
+        begin(t, 1)
+    for t in (0, 1, 2):
+        finish(t, 1)
+        begin(t, 2)
+    for t in (3, 4, 5):
+        middle(t, 1)
+    for t in (0, 1, 2):
+        middle(t, 2)
+    for t in (3, 4, 5):
+        finish(t, 1)
+        begin(t, 2)
+    for t in (0, 1, 2):
+        finish(t, 2)
+    late = ff - EARLY
+    pieces = []
     for t in range(n):
-        fill(t, 0)
-    for phase in range(3):
-        if phase:
-            for t in range(n):
-                begin(t, phase)
-        for t in range(n):
-            middle(t, phase)
-        for t in range(n):
-            finish(t, phase)
-    pieces = (
-        ((0, ff, o_gate, c * ff), (ff, half, o_in, c * half), (ff + half, 128, o_small, c * 128)),
-        ((0, ff, o_up, c * ff), (ff, half, o_in, width + c * half), (ff + half, quarter, o_out, c * half)),
-        ((0, ff, o_down, c * ff), (ff, half, o_in, 2 * width + c * half), (ff + half, quarter, o_out, c * half + quarter)),
-    )
-    other = (
-        ((o_gate, (1 - c) * ff), (o_in, (1 - c) * half), (o_small, (1 - c) * 128)),
-        ((o_up, (1 - c) * ff), (o_in, width + (1 - c) * half), (o_out, (1 - c) * half)),
-        ((o_down, (1 - c) * ff), (o_in, 2 * width + (1 - c) * half), (o_out, (1 - c) * half + quarter)),
-    )
-    slot = xh * 4 + z
+        wide = (o_gate, o_up, o_down)[t % 3]
+        if t < 3:
+            pieces.append([(0, EARLY, wide, 0, ff)])
+        else:
+            i = t - 3
+            pieces.append([(0, late, wide, EARLY, ff), (late, half, o_in, i * width, half)])
+            if i:
+                pieces[-1].append((late + half, quarter, o_out, (i - 1) * quarter, half))
+            else:
+                pieces[-1].append((late + half, 128, o_small, 0, 128))
+    base = [sum(len(p) for p in pieces[:t]) for t in range(n)]
 
     def spot(out, row, count, col, size):
         return out.at[pl.ds(pl.multiple_of(row, 16), count), pl.ds(pl.multiple_of(col, 128), size)]
 
-    keeps = []
-    for t in range(n):
-        for k, (at, size, out, col) in enumerate(pieces[t]):
+    def landing(t, k, dx, dz):
+        at, size, out, col, stride = pieces[t][k]
+        slot = (xh + dx) % 2 * 4 + (z + dz + 4) % 4
+        return spot(out, slot * 16, 16, col + c * stride, size)
+
+    def pass_on(t, k, i, src, dst, to):
+        key_ = (base[t] + k) * 7 + i
+        cp = remote(src, dst, spread_send.at[key_], spread_recv.at[key_], to)
+        cp.start()
+        pending.append(cp)
+
+    def landed(t, k, i, dx, dz):
+        key_ = (base[t] + k) * 7 + i
+        dst = landing(t, k, dx, dz)
+        remote(dst, dst, spread_send.at[key_], spread_recv.at[key_], sibling).wait_recv()
+
+    zm, zp = near["Z"]
+    keeps = {}
+
+    def spread(t):
+        for k, (at, size, out, col, stride) in enumerate(pieces[t]):
             piece = held[t].at[xl, y, xh, z, :, pl.ds(at, size)]
-            dst = spot(out, slot * 16, 16, col, size)
-            for i, to in enumerate(spread_to):
-                key_ = (t * 3 + k) * 7 + i
-                cp = remote(piece, dst, spread_send.at[key_], spread_recv.at[key_], to)
-                cp.start()
-                pending.append(cp)
-            keeps.append(pltpu.make_async_copy(piece, dst, local_sem.at[t * 3 + k]))
-            keeps[-1].start()
-    for t in range(n):
-        for k, (at, size, out, col) in enumerate(pieces[t]):
-            keeps[t * 3 + k].wait()
-            for i, (dx, dz) in enumerate(replicas):
-                src = ((xh + dx // 2) % 2) * 4 + (z + 4 - dz) % 4
-                dst = spot(out, src * 16, 16, col, size)
-                key_ = (t * 3 + k) * 7 + i
-                remote(dst, dst, spread_send.at[key_], spread_recv.at[key_], sibling).wait_recv()
-            whole = spot(out, 0, 128, col, size)
-            cp = remote(whole, whole, core_send.at[t * 3 + k], core_recv.at[t * 3 + k], sibling)
+            dst = landing(t, k, 0, 0)
+            for i, to in enumerate((across, beyond, zp, zm)):
+                pass_on(t, k, i, piece, dst, to)
+            keeps[t, k] = pltpu.make_async_copy(piece, dst, local_sem.at[base[t] + k])
+            keeps[t, k].start()
+
+    def spread_more(t):
+        for k in range(len(pieces[t])):
+            landed(t, k, 0, 1, 0)
+            mine = landing(t, k, 1, 0)
+            pass_on(t, k, 4, mine, mine, zp)
+            pass_on(t, k, 5, mine, mine, zm)
+            landed(t, k, 1, 0, 2)
+            mine = landing(t, k, 0, 2)
+            pass_on(t, k, 6, mine, mine, across)
+
+    def share(t):
+        for k, (at, size, out, col, stride) in enumerate(pieces[t]):
+            keeps[t, k].wait()
+            landed(t, k, 2, 0, -1)
+            landed(t, k, 3, 0, 1)
+            landed(t, k, 4, 1, -1)
+            landed(t, k, 5, 1, 1)
+            landed(t, k, 6, 1, 2)
+            whole = spot(out, 0, 128, col + c * stride, size)
+            cp = remote(whole, whole, core_send.at[base[t] + k], core_recv.at[base[t] + k], sibling)
             cp.start()
             pending.append(cp)
+
+    for t in (0, 1, 2):
+        spread(t)
+    for t in (3, 4, 5):
+        middle(t, 2)
+    for t in (3, 4, 5):
+        finish(t, 2)
+        spread(t)
+    for step in (spread_more, share):
+        for t in range(n):
+            step(t)
     for t in range(n):
-        for k, (out, col) in enumerate(other[t]):
-            dst = spot(out, 0, 128, col, pieces[t][k][1])
-            remote(dst, dst, core_send.at[t * 3 + k], core_recv.at[t * 3 + k], sibling).wait_recv()
+        for k, (at, size, out, col, stride) in enumerate(pieces[t]):
+            dst = spot(out, 0, 128, col + (1 - c) * stride, size)
+            remote(dst, dst, core_send.at[base[t] + k], core_recv.at[base[t] + k], sibling).wait_recv()
     for cp in pending:
         cp.wait_send()
 
 
-def reduce_grads(act_mid, gg, act_in, gproj, small, gu, gated, gmix, cot, hidden):
+def reduce_grads(mid_t, gg, in_t, gproj, small, gu, gated, gmix, cot_t, hidden, *begun):
     n = COUNT
-    ins = (act_mid, gg, act_in, gproj, small, gu, gated, gmix, cot, hidden)
-    width, ff, two = act_in.shape[1], gg.shape[1], act_in.shape[0]
+    ins = (mid_t, gg, in_t, gproj, small, gu, gated, gmix, cot_t, hidden)
+    width, ff, two = gated.shape[1], gg.shape[1], gated.shape[0]
     half = width // 2
-    widths = (ff + half + 128, ff + half + half // 2, ff + half + half // 2)
+    late = ff - EARLY + half
+    widths = (EARLY,) * 3 + (late + 128, late + half // 2, late + half // 2)
     lead = (2, 4, 2, 4, 16)
     held = [pltpu.VMEM(lead + (w,), BF) for w in widths]
     relay, takes = [], []
@@ -811,7 +995,7 @@
                 relay.append(pltpu.VMEM(dims + (16, halves(widths[t])[h][1]), BF))
                 takes.append(pltpu.VMEM(dims + (16, widths[t]), BF))
     bufs = [pltpu.VMEM(a.shape, a.dtype) for a in ins]
-    turned = [pltpu.VMEM(lead + (two,), BF)] * 4
+    turned = [pltpu.VMEM(lead + (two,), BF)]
     dma = pltpu.SemaphoreType.DMA
     hbm = pl.BlockSpec(memory_space=pltpu.HBM)
     rows = 128
@@ -819,20 +1003,20 @@
     return pl.pallas_call(
         reduce_kernel,
         out_shape=tuple(jax.ShapeDtypeStruct((rows, w), BF) for w in outs),
-        in_specs=[hbm] * len(ins),
+        in_specs=[hbm] * len(ins + begun),
         out_specs=(hbm,) * len(outs),
         scratch_shapes=held + relay + takes + bufs + turned
-        + [dma((10,)), dma((54,)), dma((54,)), dma((63,)), dma((63,)), dma((9,)), dma((9,))],
+        + [dma((19,)), dma((108,)), dma((108,)), dma((84,)), dma((84,)), dma((12,)), dma((12,))],
         compiler_params=pltpu.CompilerParams(collective_id=2, has_side_effects=True, vmem_limit_bytes=62 << 20),
-    )(*ins)
+    )(*ins, *begun)
 
 
 def local(tokens, norm_in, w_in, conv_w, w_out, norm_mid, w_gate, w_up, w_down, cotangent):
     gains = jnp.stack([norm_in, norm_mid])
     (
-        result, grad_tokens, act_in, act_mid, hidden, gg, gu, gproj, gated, gmix, cot, small
+        result, grad_tokens, in_t, mid_t, hidden, gg, gu, gproj, gated, gmix, cot_t, small, *begun
     ) = block_call(tokens[0], cotangent[0], w_in, w_out, w_gate, w_up, w_down, gains, conv_w.T)
-    sums = reduce_grads(act_mid, gg, act_in, gproj, small, gu, gated, gmix, cot, hidden)
+    sums = reduce_grads(mid_t, gg, in_t, gproj, small, gu, gated, gmix, cot_t, hidden, *begun)
     g_gate, g_up, g_down, g_in, g_out, g_small = (s.astype(F32) for s in sums)
     g_small = g_small[:, :128] + g_small[:, 128:]
     return (

time: 315 us -> 239 us (0.76)
  Pallas kernels: 300 us -> 222 us
    pallas_call x1, Pallas kernels: 139 us -> 86.6 us  [reduce_grads(): pl.pallas_call(reduce_kernel, out_shape=tuple((jax.ShapeDtypeStruct((rows...]
    pallas_call x1, Pallas kernels: 162 us -> 136 us  [block_call(): pl.pallas_call(block_kernel, out_shape=(out(length, width), out(length, w...]
where the time goes in v1:
time: 239 us; the launch traced here: 237 us
  Pallas kernels  222 us (93%)
  other arithmetic  10.2 us (4%)
  local copies, waits for them, and re-layouts  3.22 us (1%)
    pallas_call x1, Pallas kernels, block_call(): pl.pallas_call(block_kernel, out_shape=(out(length, width), out(length, w...  136 us
    pallas_call x1, Pallas kernels, reduce_grads(): pl.pallas_call(reduce_kernel, out_shape=tuple((jax.ShapeDtypeStruct((rows...  86.6 us
    convert_element_type x6, other arithmetic, local(): g_gate, g_up, g_down, g_in, g_out, g_small = (s.astype(F32) for s in sums)  9.03 us

profile of v1, /device:TPU:27, one launch (start us, length us, event | category | flops | bytes accessed | tf_op | source)
XLA Modules:
  0.0 236.6 jit_solution(17643954253117907689)
XLA Ops:
  0.6 1.2 pad_maximum_fusion.gains
  1.8 135.9 %shard_map.177 = (bf16[256,1024]{1,0:T(8,128)(2,1)}, f32[256,1024]{1,0:T(8,128)}, bf16[2,4,2,4,16,512]{5,4,3,2,1,0:T(8,128)(2,1)}, bf16[2,4,2,4,16,512]{5,4,3,2,...) custom-call(bf16[256,1024]{1,0:T(8,128)(2,1)} %bitcast.8, ...), custom_call_target="tpu_custom_call" | custom-call | tf_op jit(solution)/shard_map/pallas_call | solution.py:662
  137.7 86.6 %shard_map.178 = (bf16[128,4608]{1,0:T(8,128)(2,1)}, bf16[128,4608]{1,0:T(8,128)(2,1)}, bf16[128,4608]{1,0:T(8,128)(2,1)}, bf16[128,3072]{1,0:T(8,128)(2,1)}, bf...) custom-call(bf16[2,4,2,4,16,512]{5,4,3,2,1,0:T(8,128)(2,1)} %get-tuple-element.39.refs_0_, ...), custom_call_target="tpu_custom_call" | custom-call | tf_op jit(solution)/shard_map/pallas_call | solution.py:1003
  224.3 0.0 copy-start.4
  224.3 0.9 convert_element_type.18
  225.2 0.7 slice_reduce_fusion
  225.9 0.1 slice.23
  226.0 0.7 copy.21
  226.7 0.0 copy-start.2
  226.7 1.9 convert_element_type.20
  228.6 0.0 copy-done.4
  228.6 1.3 convert_element_type.19
  229.9 0.0 copy-done.2
  229.9 0.0 copy-start.1
  229.9 1.6 convert_element_type.21
  231.5 0.0 copy-done.1
  231.5 0.0 copy-start
  231.5 1.6 convert_element_type.22
  233.2 0.0 copy-done
  233.2 0.0 copy-start.5
  233.2 0.0 copy-start.3
  233.2 1.6 convert_element_type.23
  234.8 0.0 copy-done.5
  234.8 0.8 copy.24
  235.6 0.0 copy-done.3
  235.6 1.0 copy.25
  (1 shorter events, 0.0 us)
Async XLA Ops:
  224.3 4.3 %copy-start.4 = (bf16[128,3072]{1,0:T(8,128)(2,1)S(1)}, bf16[128,3072]{1,0:T(8,128)(2,1)}, u32[]{:S(2)}) copy-start(bf16[128,3072]{1,0:T(8,128)(2,1)} %get-tuple-element.59) | copy-start | bytes 2359300
  226.7 3.2 %copy-start.2 = (bf16[128,4608]{1,0:T(8,128)(2,1)S(1)}, bf16[128,4608]{1,0:T(8,128)(2,1)}, u32[]{:S(2)}) copy-start(bf16[128,4608]{1,0:T(8,128)(2,1)} %get-tuple-element.61) | copy-start | bytes 3538948
  229.9 1.6 copy-start.1
  231.5 1.6 copy-start
  233.2 1.6 copy-start.5
  233.2 2.4 %copy-start.3 = (f32[256,1024]{1,0:T(8,128)S(1)}, f32[256,1024]{1,0:T(8,128)}, u32[]{:S(2)}) copy-start(f32[256,1024]{1,0:T(8,128)} %get-tuple-element.38) | copy-start | bytes 3145732

commit v2 on v1

--- a/solution.py
+++ b/solution.py
@@ -87,8 +87,8 @@
     return (0, first), (first, columns - first)
 
 
-EARLY = 1536
-WIDE = 768
+EARLY = 2048
+WIDE = 1024
 LEAD = (2, 4, 2, 4, 16)
 
 
@@ -114,19 +114,21 @@
     loop(source.shape[0] // size, one)
 
 
-SWAPS = ("tokens", "cot", "gated0", "gated1", "mix", "act", "ffn", "gam", "gmix", "gai", "fore", "back")
+SWAPS = ("tokens", "cot", "gated0", "gated1", "mix", "act", "gam", "gmix", "fore", "back")
 TILE = 256
 
 
 def block_kernel(
     tokens, cot, w_in, w_out, w_gate, w_up, w_down, gains, taps_in,
-    result, grad_tokens, o_in_t, o_mid_t, o_hidden, o_gg, o_gu, o_proj, o_gated, o_mix, o_cot_t, o_small,
-    own0, left0, right0, own1, left1, right1, own2, left2, right2,
-    win, wout, wgu, wd, ext, tok2, cot2, act_in, proj, mixed, conv, gated, part, box_mix, box_ffn, box_gam, box_gai,
-    resid, normed, act_mid, hidden, held, gg, gu, gmix, gconv, gproj, vecs, small, scale_mid, out_res, mid_t, cot_t,
-    far_a0, far_b0, far_a1, far_b1, far_a2, far_b2,
+    o_win, o_wd, o_resid, o_grad_resid, o_vecs,
+    o_in_t, o_mid_t, o_hidden, o_gg, o_gu, o_proj, o_gated, o_mix, o_cot_t, o_small, *rest,
+):
+    begun, rest = [rest[7 * t : 7 * t + 7] for t in range(3)], rest[21:]
+    (
+        win, wout, wgu, wd, ext, tok2, cot2, act_in, proj, mixed, conv, gated, part, box_mix, box_gam,
+    resid, normed, act_mid, hidden, held, gg, gu, gmix, gconv, gproj, vecs, small, scale_mid, mid_t, cot_t,
     local_sem, send_sem, recv_sem, core_send, core_recv, out_sem, early_send, early_recv,
-):
+    ) = rest
     xl, xh, y, z, c = place()
     x = xh * 2 + xl
     shard, replica = lax.axis_index("shard"), lax.axis_index("replica")
@@ -165,9 +167,26 @@
         used.append(dst)
         stores[-1].start()
 
+    ending = []
+
     def fire(cp):
-        cp.start()
-        pending.append(cp.wait_send)
+        if ending:
+            cp.wait_send()
+        else:
+            cp.start()
+            pending.append(cp.wait_send)
+
+    owner = c == xl
+
+    def only(condition, *bodies):
+        before = len(pending)
+
+        @pl.when(condition)
+        def _():
+            for body in bodies:
+                body(WOUT)
+
+        del pending[before:]
 
     def swap(name, src, dst, to=None):
         k = SWAPS.index(name)
@@ -203,6 +222,8 @@
         fire(remote(view, view, send_sem.at[k], recv_sem.at[k], to))
 
     def got(view, k):
+        if ending:
+            return
         remote(view, view, send_sem.at[k], recv_sem.at[k], yp).wait_recv()
 
     def cut(view, h):
@@ -285,7 +306,7 @@
     fire(swap("cot", cot2.at[lower], cot2.at[upper]))
     for cp in loads[5:7]:
         cp.wait()
-    launch_x(WOUT)
+    only(owner, launch_x)
     launch_x(WDZ)
     launch_x(WDX)
     for stage in (stage_a, stage_b, stage_c):
@@ -308,12 +329,12 @@
     in_store = stores.pop()
     stage_c(WGU, 0)
     stage_a(WGU)
-    launch_y(WOUT)
+    only(owner, launch_y)
     stage_a(WIN)
     launch_y(WDZ)
     stage_c(WGU, -1, 1)
     stage_b(WGU)
-    stage_a(WOUT)
+    only(owner, stage_a)
     launch_y(WDX)
     stage_b(WIN)
     stage_c(WGU, 2)
@@ -326,6 +347,8 @@
     def proj_step(j):
         proj[:, chunk(j, TILE)] = mul(act_in[...], flat(win[:, :, chunk(j, TILE)]))
 
+    store(win, o_win)
+    store(vecs, o_vecs)
     loop(3 * half // TILE, proj_step)
 
     def b_of(at):
@@ -350,7 +373,7 @@
     def _():
         fore.start()
 
-    stage_b(WOUT)
+    only(owner, stage_b)
     stage_c(WDZ, 0)
     stage_a(WDX)
 
@@ -376,7 +399,7 @@
     fire(swap("gated1", gated_mine.at[upper], gated_mine.at[lower]))
     stage_b(WDZ)
     stage_c(WDZ, -1, 1)
-    stage_c(WOUT)
+    only(jnp.logical_not(owner), stage_c)
     wout_mine = wout.at[pl.ds(pl.multiple_of(c * 4, 4), 4)]
 
     def mix_step(j):
@@ -398,6 +421,7 @@
         act_mid[at] = (n * vecs[1:2]).astype(BF)
 
     loop(length // rc, norm_mid_step)
+    store(resid, o_resid)
     act_swap = swap("act", act_mid.at[lower], act_mid.at[upper])
     act_swap.start()
     stage_c(WDZ, 2)
@@ -409,8 +433,6 @@
 
     where = {"X": x, "Y": y, "Z": z}
     near = {"X": (xm, xp), "Y": (ym, yp), "Z": (zm, zp)}
-    landings = ((own0, left0, right0), (own1, left1, right1), (own2, left2, right2))
-    relays = ((far_a0, far_b0), (far_a1, far_b1), (far_a2, far_b2))
     eh = EARLY // 2
 
     def early_at(t, step):
@@ -431,14 +453,19 @@
     def early_cols(view, h):
         return view.at[(slice(None),) * (len(view.shape) - 1) + (pl.ds(h * eh, eh),)]
 
+    def keep(t):
+        store(held.at[(t,) + early_at(t, 0)], begun[t][0])
+        store(early_cols(held.at[(t,) + early_at(t, 1)], 0), begun[t][1])
+        store(early_cols(held.at[(t,) + early_at(t, 3)], 1), begun[t][2])
+
     def early_copy(t, k):
-        to_right = k in (0, 2, 4)
-        h = (0, 1, 1, 0, 0, 1)[k]
+        to_right = k in (0, 2)
+        h = (0, 1, 1, 0)[k]
         step = 2 if k < 2 else (1 if to_right else 3)
         src = early_cols(held.at[(t,) + early_at(t, step)], h)
-        dst = relays[t][k] if k < 2 else early_cols(landings[t][1 if to_right else 2], h)
+        dst = begun[t][3 + k]
         to = near[ORDERS[t][0]][1 if to_right else 0]
-        return remote(src, dst, early_send.at[t * 6 + k], early_recv.at[t * 6 + k], to)
+        return remote(src, dst, early_send.at[t * 4 + k], early_recv.at[t * 4 + k], to)
 
     def gate_step(j):
         at = chunk(j, TILE)
@@ -448,9 +475,9 @@
         silu = gate * sig
         hidden[:, at] = (silu * up).astype(BF)
         factor = up * (sig * (1.0 + gate * (1.0 - sig)))
-        spot = (slice(None),) * 4 + (chunk(j % 6, TILE),)
-        held[(j // 6, 0) + spot] = factor.astype(BF).reshape(LEAD[1:] + (TILE,))
-        held[(j // 6, 1) + spot] = silu.astype(BF).reshape(LEAD[1:] + (TILE,))
+        spot = (slice(None),) * 4 + (chunk(j % (EARLY // TILE), TILE),)
+        held[(j // (EARLY // TILE), 0) + spot] = factor.astype(BF).reshape(LEAD[1:] + (TILE,))
+        held[(j // (EARLY // TILE), 1) + spot] = silu.astype(BF).reshape(LEAD[1:] + (TILE,))
 
     loop(ff // TILE, gate_step)
     store(hidden, o_hidden)
@@ -462,20 +489,21 @@
     early_fill(2, 3)
     fire(early_copy(2, 3))
     early_fill(2, 0)
-    store(held.at[(2,) + early_at(2, 0)], landings[2][0])
+    keep(2)
     stage_c(WDX)
     stage_d(WDZ)
 
     def grad_hidden_step(j):
         at = chunk(j, TILE)
         g = mul(cot2[...], flat(wd[:, :, at]))
-        spot = (slice(None),) * 4 + (chunk(j % 6, TILE),)
-        gg[:, at] = (g * flat(held[(j // 6, 0) + spot]).astype(F32)).astype(BF)
-        gu[:, at] = (g * flat(held[(j // 6, 1) + spot]).astype(F32)).astype(BF)
+        spot = (slice(None),) * 4 + (chunk(j % (EARLY // TILE), TILE),)
+        gg[:, at] = (g * flat(held[(j // (EARLY // TILE), 0) + spot]).astype(F32)).astype(BF)
+        gu[:, at] = (g * flat(held[(j // (EARLY // TILE), 1) + spot]).astype(F32)).astype(BF)
 
     loop(ff // TILE, grad_hidden_step)
-    store(gg, o_gg)
-    store(gu, o_gu)
+    store(gg.at[:, pl.ds(EARLY, ff - EARLY)], o_gg)
+    store(gu.at[:, pl.ds(EARLY, ff - EARLY)], o_gu)
+    store(wd, o_wd)
     for t in (0, 1):
         early_fill(t, 2)
         fire(early_copy(t, 0))
@@ -511,7 +539,7 @@
     gmix_swap.start()
     for t in (0, 1):
         early_fill(t, 0)
-        store(held.at[(t,) + early_at(t, 0)], landings[t][0])
+        keep(t)
     gam_swap.wait_send()
 
     def ffn_step(j):
@@ -519,35 +547,7 @@
         part[:, chunk(j, TILE)] = times_rows(hidden[...], flat(wd[u]))
 
     loop(4, ffn_step)
-    for t in range(3):
-        for k in (0, 1):
-            early_copy(t, k).wait_recv()
-            at = early_at(t, (1, 3)[k])
-            box = relays[t][k]
-            dims = dims_left(ORDERS[t], 0)
-            total = dims[0] * dims[1] * (dims[2] if len(dims) > 2 else 1)
-
-            def add(i, at=at, box=box, dims=dims, t=t, k=k):
-                places, rest = [], i
-                for d in reversed(dims):
-                    places.append(rest % d)
-                    rest = rest // d
-                places = tuple(reversed(places))
-                left_over = iter(places)
-                spot = (t,) + tuple(next(left_over) if isinstance(a, slice) else a for a in at)
-                spot = spot + (slice(None), pl.ds(k * eh, eh))
-                held[spot] = (held[spot].astype(F32) + box[places].astype(F32)).astype(BF)
-
-            loop(total, add)
-            fire(early_copy(t, 4 + k))
-    ffn_swap = swap("ffn", part.at[upper], box_ffn)
-    ffn_swap.start()
-
-    def own_ffn_step(i):
-        at = chunk(i, rc)
-        resid[at] = resid[at] + part[at]
-
-    loop(length // rc, own_ffn_step)
+    store(box_gam, o_grad_resid)
     gmix_swap.wait_recv()
     for q in (0, 1):
         box_mix[:, pl.ds(q * half, half)] = times_rows(gmix[pl.ds(q * length, length)], flat(wout_mine[...]))
@@ -583,48 +583,22 @@
             gproj[at, pl.ds(2 * half, half)] = (gm * b_of(at)).astype(BF)
 
     loop(length // rc, gproj_step)
-    ffn_swap.wait_send()
-
-    def gai_step(j):
-        u = pl.ds(j * 2, 2)
-        part[:, chunk(j, TILE)] = times_rows(gproj[...], flat(win[u]))
-
-    loop(4, gai_step)
-    gai_swap = swap("gai", part.at[upper], box_gai)
-    gai_swap.start()
-    ffn_swap.wait_recv()
-
-    def result_step(i):
-        at = chunk(i, rc)
-        out_res[at] = (resid[at] + box_ffn[at]).astype(BF)
-
-    loop(length // rc, result_step)
     swap("gated0", gated_other.at[upper], gated_other.at[upper]).wait_recv()
     swap("gated1", gated_other.at[lower], gated_other.at[lower]).wait_recv()
     store(gproj, o_proj)
     store(gated, o_gated)
     store(gmix, o_mix)
-    store(out_res, result)
-    gai_swap.wait_recv()
-
-    def final_step(i):
-        at = chunk(i, rc)
-        g = part[at] + box_gai[at]
-        n, s = normalize(tok2[at].astype(F32))
-        small[0:1] = small[0:1] + jnp.sum(g * n, axis=0, keepdims=True)
-        resid[at] = box_gam[at] + norm_back(g * vecs[0:1], n, s)
-
-    loop(length // rc, final_step)
-    store(resid, grad_tokens)
     store(small, o_small)
     for t in range(3):
-        for k in (2, 3, 4, 5):
+        for k in range(4):
             early_copy(t, k).wait_recv()
     for wait in pending:
         wait()
+
+    ending.append(True)
+    only(owner, launch_x, launch_y, stage_a, stage_b)
     act_swap.wait_send()
     gmix_swap.wait_send()
-    gai_swap.wait_send()
 
     @pl.when(jnp.logical_not(last))
     def _():
@@ -656,53 +630,56 @@
         return pltpu.VMEM(shape, dtype)
 
     firsts = [dims_left(ORDERS[t], 0) + (16,) for t in range(3)]
-    early = [out(*firsts[t], EARLY) for t in range(3) for _ in range(3)]
-    relays = [mem(*firsts[t], EARLY // 2) for t in range(3) for _ in range(2)]
+    early = [out(*firsts[t], EARLY if k == 0 else EARLY // 2) for t in range(3) for k in range(7)]
     dma = pltpu.SemaphoreType.DMA
     return pl.pallas_call(
         block_kernel,
         out_shape=(
-            out(length, width), out(length, width, dtype=F32), out(*LEAD, two), out(*LEAD, two), out(two, ff),
-            out(two, ff), out(two, ff), out(two, 3 * half), out(two, width), out(two, width), out(*LEAD, two),
+            out(8, rows, 3 * half), out(8, rows, ff), out(length, width, dtype=F32), out(length, width, dtype=F32),
+            out(16, width, dtype=F32), out(*LEAD, two), out(*LEAD, two), out(two, ff),
+            out(two, ff - EARLY), out(two, ff - EARLY), out(two, 3 * half), out(two, width), out(two, width), out(*LEAD, two),
             out(8, width, dtype=F32), *early,
         ),
         in_specs=[hbm] * 7 + [vm] * 2,
-        out_specs=(hbm,) * 21,
+        out_specs=(hbm,) * 36,
         scratch_shapes=[
             mem(8, rows, 3 * half), mem(8, rows, width), mem(2, 8, rows, ff), mem(8, rows, ff), mem(8, 32, 128),
             mem(two, width), mem(two, width), mem(two, width), mem(two, 3 * half, dtype=F32),
             mem(2, length + 8, half, dtype=F32), mem(two, half, dtype=F32), mem(two, width), mem(two, width, dtype=F32),
             mem(length, width, dtype=F32), mem(length, width, dtype=F32), mem(length, width, dtype=F32),
-            mem(length, width, dtype=F32), mem(length, width, dtype=F32), mem(length, width, dtype=F32), mem(two, width),
+            mem(length, width, dtype=F32), mem(two, width),
             mem(two, ff), mem(3, *LEAD, EARLY), mem(two, ff), mem(two, ff), mem(two, width),
             mem(2, length + 8, half, dtype=F32), mem(two, 3 * half), mem(16, width, dtype=F32), mem(8, width, dtype=F32),
-            mem(length, 128, dtype=F32), mem(length, width), mem(*LEAD, two), mem(*LEAD, two), *relays,
-            dma((9,)), dma((COPIES,)), dma((COPIES,)), dma((len(SWAPS),)), dma((len(SWAPS),)), dma((15,)), dma((18,)), dma((18,)),
+            mem(length, 128, dtype=F32), mem(*LEAD, two), mem(*LEAD, two),
+            dma((9,)), dma((COPIES,)), dma((COPIES,)), dma((len(SWAPS),)), dma((len(SWAPS),)), dma((48,)), dma((12,)), dma((12,)),
         ],
         compiler_params=pltpu.CompilerParams(collective_id=1, has_side_effects=True, vmem_limit_bytes=62 << 20),
     )(tokens, cot, w_in, w_out, w_gate, w_up, w_down, gains, taps)
 COUNT = 6
+INS = 16
 
 
 def reduce_kernel(*refs):
     n = COUNT
-    ins, refs = refs[:10], refs[10:]
-    begun, refs = refs[:9], refs[9:]
-    outs, refs = refs[:6], refs[6:]
+    ins, refs = refs[:INS], refs[INS:]
+    begun, refs = refs[:21], refs[21:]
+    outs, refs = refs[:8], refs[8:]
     held, refs = refs[:n], refs[n:]
     relay, refs = [refs[6 * t : 6 * t + 6] for t in range(n)], refs[6 * n :]
     takes, refs = [refs[6 * t : 6 * t + 6] for t in range(n)], refs[6 * n :]
-    bufs, refs = refs[:10], refs[10:]
+    bufs, refs = refs[:INS], refs[INS:]
     turned, refs = refs[:1], refs[1:]
+    (sums, box_ffn, box_gai, out_res), refs = refs[:4], refs[4:]
     local_sem, send_sem, recv_sem, spread_send, spread_recv, core_send, core_recv = refs
-    o_gate, o_up, o_down, o_in, o_out, o_small = outs
+    o_gate, o_up, o_down, o_in, o_out, o_small, result, grad_tokens = outs
     xl, xh, y, z, c = place()
     x = xh * 2 + xl
     loads = [pltpu.make_async_copy(a, b, local_sem.at[i]) for i, (a, b) in enumerate(zip(ins, bufs))]
-    mid_t, gg, in_t, gproj, small, gu, gated, gmix, cot_t, hidden = bufs
+    in_t, gproj, cot_t, hidden, gated, gmix, mid_t, gu, win, grad_resid, vecs, tokens, small, gg, wd, resid = bufs
     (gated_t,) = turned
     half = gproj.shape[1] // 3
-    ff = gg.shape[1]
+    ff = hidden.shape[1]
+    length = tokens.shape[0]
     width = half * 2
     quarter = half // 2
     where = {"X": x, "Y": y, "Z": z}
@@ -713,10 +690,24 @@
     }
     taken = []
     for t in range(3):
-        at = quarter_at(ORDERS[t][0], where[ORDERS[t][0]])
-        boxes = (held[t].at[at], takes[t][0], takes[t][1])
-        taken += [pltpu.make_async_copy(begun[3 * t + k], boxes[k], local_sem.at[10 + 3 * t + k]) for k in range(3)]
-    for cp in (*loads, *taken):
+        axis = ORDERS[t][0]
+        p, low, high = where[axis], pl.ds(0, EARLY // 2), pl.ds(EARLY // 2, EARLY // 2)
+        lead = (slice(None),) * len(dims_left(axis, 0)) + (slice(None),)
+        boxes = (
+            held[t].at[quarter_at(axis, p)],
+            held[t].at[quarter_at(axis, (p + 1) % 4)].at[lead + (low,)],
+            held[t].at[quarter_at(axis, (p + 3) % 4)].at[lead + (high,)],
+            relay[t][0],
+            relay[t][1],
+            takes[t][0].at[lead + (high,)],
+            takes[t][1].at[lead + (low,)],
+        )
+        for k in (1, 2, 3, 4, 0, 5, 6):
+            i = 7 * t + k
+            taken.append(pltpu.make_async_copy(begun[i], boxes[k], local_sem.at[INS + i]))
+    firsts = [cp for t in range(3) for cp in taken[7 * t : 7 * t + 4]]
+    others = [cp for t in range(3) for cp in taken[7 * t + 4 : 7 * t + 7]]
+    for cp in (*firsts, *loads[:8], *others, *loads[8:]):
         cp.start()
     across, beyond = device(x + 2, y, z, c), device(x, y, z + 2, c)
     sibling = device(x, y, z, 1 - c)
@@ -800,8 +791,13 @@
         left, right = near[order[phase]]
         ra, rb, tl, tr = buffers(t, phase)
         dims = dims_left(order, phase)
+        begun_here = t < 3 and phase == 0
+        if begun_here:
+            for cp in taken[7 * t : 7 * t + 4]:
+                cp.wait()
         for h, (box, q, to, dst) in enumerate(((ra, (p + 1) % 4, right, tl), (rb, (p + 3) % 4, left, tr))):
-            arrived(box, t, phase, h)
+            if not begun_here:
+                arrived(box, t, phase, h)
             at0, size = halves(held[t].shape[-1])[h]
 
             def add(at, box=box, q=q, at0=at0, size=size):
@@ -817,13 +813,13 @@
         ra, rb, tl, tr = buffers(t, phase)
         dims = dims_left(order, phase)
         if t < 3 and phase == 0:
-            for cp in taken[3 * t : 3 * t + 3]:
+            for cp in taken[7 * t + 4 : 7 * t + 7]:
                 cp.wait()
         else:
             arrived(cols(tl, 1, t), t, phase, 2)
             arrived(cols(tr, 0, t), t, phase, 3)
-            arrived(cols(tl, 0, t), t, phase, 4)
-            arrived(cols(tr, 1, t), t, phase, 5)
+        arrived(cols(tl, 0, t), t, phase, 4)
+        arrived(cols(tr, 1, t), t, phase, 5)
 
         def add(at):
             slab = full(order, phase, p, at)
@@ -846,42 +842,91 @@
 
         i = t % 3
         left, right = (mid_t, mid_t, cot_t)[i], (gg, gu, hidden)[i]
-        block(left, right, EARLY, ff - EARLY, 0)
+        block(left, right, EARLY if i == 2 else 0, ff - EARLY, 0)
         block(in_t, gproj, i * half, half, ff - EARLY)
         if i:
             block(gated_t, gmix, c * half + (i - 1) * quarter, quarter, ff - EARLY + half)
 
-    for cp in loads[:5]:
+    def swap(k, dst):
+        return remote(sums.at[pl.ds(length, length)], dst, core_send.at[12 + k], core_recv.at[12 + k], sibling)
+
+    def gai_step(j):
+        sums[:, chunk(j, TILE)] = times_rows(gproj[...], flat(win[pl.ds(j * 2, 2)]))
+
+    def ffn_step(j):
+        sums[:, chunk(j, TILE)] = times_rows(hidden[...], flat(wd[pl.ds(j * 2, 2)]))
+
+    def final_step(i):
+        at = chunk(i, 32)
+        g = sums[at] + box_gai[at]
+        normed, scale = normalize(tokens[at].astype(F32))
+        small[0:1] = small[0:1] + jnp.sum(g * normed, axis=0, keepdims=True)
+        grad_resid[at] = grad_resid[at] + norm_back(g * vecs[0:1], normed, scale)
+
+    def own_ffn_step(i):
+        at = chunk(i, 32)
+        resid[at] = resid[at] + sums[at]
+
+    def result_step(i):
+        at = chunk(i, 32)
+        out_res[at] = (resid[at] + box_ffn[at]).astype(BF)
+
+    for t in (0, 1, 2):
+        middle(t, 0)
+    for cp in loads[:6]:
         cp.wait()
+    turn(gated, gated_t)
+    fill(5, 2)
+    begin(5, 0, second=False)
+    for cp in loads[6:9]:
+        cp.wait()
+    loop(4, gai_step)
+    gai_swap = swap(0, box_gai)
+    gai_swap.start()
+    fill(4, 2)
+    begin(4, 0, second=False)
+    for t in (5, 4):
+        fill(t, 1)
+        fill(t, 3)
+        begin(t, 0, first=False)
+    for cp in loads[9:]:
+        cp.wait()
+    gai_swap.wait_recv()
+    loop(length // 32, final_step)
+    back = [pltpu.make_async_copy(grad_resid, grad_tokens, local_sem.at[INS + 21])]
+    back[0].start()
     tall = jnp.concatenate([small[...], jnp.zeros((120, width), F32)], axis=0)
     held[3][:, :, :, :, :, pl.ds(ff - EARLY + half, 128)] = tall.T.astype(BF).reshape(2, 4, 2, 4, 16, 128)
     fill(3, 2)
     begin(3, 0, second=False)
-    for cp in loads[5:]:
-        cp.wait()
-    turn(gated, gated_t)
-    for t in (4, 5):
-        fill(t, 2)
-        begin(t, 0, second=False)
+    fill(3, 1)
+    fill(3, 3)
+    begin(3, 0, first=False)
+    middle(5, 0)
+    middle(4, 0)
     for t in (0, 1, 2):
         finish(t, 0)
         begin(t, 1)
-    for t in (3, 4, 5):
-        fill(t, 1)
-        fill(t, 3)
-        begin(t, 0, first=False)
+    middle(3, 0)
+    for t in (5, 4, 3):
+        fill(t, 0)
     for t in (0, 1, 2):
         middle(t, 1)
-    for t in (3, 4, 5):
-        middle(t, 0)
-    for t in (3, 4, 5):
-        fill(t, 0)
-    for t in (3, 4, 5):
+    gai_swap.wait_send()
+    loop(4, ffn_step)
+    ffn_swap = swap(1, box_ffn)
+    ffn_swap.start()
+    loop(length // 32, own_ffn_step)
+    for t in (5, 4, 3):
         finish(t, 0)
         begin(t, 1)
     for t in (0, 1, 2):
         finish(t, 1)
         begin(t, 2)
+    ffn_swap.wait_recv()
+    loop(length // 32, result_step)
+    back.append(pltpu.make_async_copy(out_res, result, local_sem.at[INS + 22]))
+    back[1].start()
     for t in (3, 4, 5):
         middle(t, 1)
     for t in (0, 1, 2):
@@ -974,14 +1019,18 @@
         for k, (at, size, out, col, stride) in enumerate(pieces[t]):
             dst = spot(out, 0, 128, col + (1 - c) * stride, size)
             remote(dst, dst, core_send.at[base[t] + k], core_recv.at[base[t] + k], sibling).wait_recv()
+    for cp in back:
+        cp.wait()
+    ffn_swap.wait_send()
     for cp in pending:
         cp.wait_send()
 
 
-def reduce_grads(mid_t, gg, in_t, gproj, small, gu, gated, gmix, cot_t, hidden, *begun):
+def reduce_grads(tokens, win, wd, resid, grad_resid, vecs, in_t, mid_t, hidden, gg, gu, gproj, gated, gmix, cot_t, small, *begun):
     n = COUNT
-    ins = (mid_t, gg, in_t, gproj, small, gu, gated, gmix, cot_t, hidden)
-    width, ff, two = gated.shape[1], gg.shape[1], gated.shape[0]
+    ins = (in_t, gproj, cot_t, hidden, gated, gmix, mid_t, gu, win, grad_resid, vecs, tokens, small, gg, wd, resid)
+    width, ff, two = gated.shape[1], hidden.shape[1], gated.shape[0]
+    length = two // 2
     half = width // 2
     late = ff - EARLY + half
     widths = (EARLY,) * 3 + (late + 128, late + half // 2, late + half // 2)
@@ -996,27 +1045,28 @@
                 takes.append(pltpu.VMEM(dims + (16, widths[t]), BF))
     bufs = [pltpu.VMEM(a.shape, a.dtype) for a in ins]
     turned = [pltpu.VMEM(lead + (two,), BF)]
+    one = pltpu.VMEM((length, width), F32)
+    own = [pltpu.VMEM((two, width), F32), one, one, pltpu.VMEM((length, width), BF)]
     dma = pltpu.SemaphoreType.DMA
     hbm = pl.BlockSpec(memory_space=pltpu.HBM)
     rows = 128
     outs = (2 * ff, 2 * ff, 2 * ff, 3 * width, width, 256)
     return pl.pallas_call(
         reduce_kernel,
-        out_shape=tuple(jax.ShapeDtypeStruct((rows, w), BF) for w in outs),
+        out_shape=tuple(jax.ShapeDtypeStruct((rows, w), BF) for w in outs)
+        + (jax.ShapeDtypeStruct((length, width), BF), jax.ShapeDtypeStruct((length, width), F32)),
         in_specs=[hbm] * len(ins + begun),
-        out_specs=(hbm,) * len(outs),
-        scratch_shapes=held + relay + takes + bufs + turned
-        + [dma((19,)), dma((108,)), dma((108,)), dma((84,)), dma((84,)), dma((12,)), dma((12,))],
+        out_specs=(hbm,) * 8,
+        scratch_shapes=held + relay + takes + bufs + turned + own
+        + [dma((39,)), dma((108,)), dma((108,)), dma((84,)), dma((84,)), dma((14,)), dma((14,))],
         compiler_params=pltpu.CompilerParams(collective_id=2, has_side_effects=True, vmem_limit_bytes=62 << 20),
     )(*ins, *begun)
 
 
 def local(tokens, norm_in, w_in, conv_w, w_out, norm_mid, w_gate, w_up, w_down, cotangent):
     gains = jnp.stack([norm_in, norm_mid])
-    (
-        result, grad_tokens, in_t, mid_t, hidden, gg, gu, gproj, gated, gmix, cot_t, small, *begun
-    ) = block_call(tokens[0], cotangent[0], w_in, w_out, w_gate, w_up, w_down, gains, conv_w.T)
-    sums = reduce_grads(mid_t, gg, in_t, gproj, small, gu, gated, gmix, cot_t, hidden, *begun)
+    kept = block_call(tokens[0], cotangent[0], w_in, w_out, w_gate, w_up, w_down, gains, conv_w.T)
+    *sums, result, grad_tokens = reduce_grads(tokens[0], *kept)
     g_gate, g_up, g_down, g_in, g_out, g_small = (s.astype(F32) for s in sums)
     g_small = g_small[:, :128] + g_small[:, 128:]
     return (

time: 239 us -> 226 us (0.946)
  Pallas kernels: 222 us -> 210 us
    pallas_call x1, Pallas kernels: 136 us -> 125 us  [block_call(): pl.pallas_call(block_kernel, out_shape=(out(8, rows, 3 * half), out(8, ro...]
where the time goes in v2:
time: 226 us; the launch traced here: 224 us
  Pallas kernels  210 us (93%)
  other arithmetic  10.2 us (5%)
  local copies, waits for them, and re-layouts  3.22 us (1%)
    pallas_call x1, Pallas kernels, block_call(): pl.pallas_call(block_kernel, out_shape=(out(8, rows, 3 * half), out(8, ro...  125 us
    pallas_call x1, Pallas kernels, reduce_grads(): pl.pallas_call(reduce_kernel, out_shape=tuple((jax.ShapeDtypeStruct((rows...  85.2 us
    convert_element_type x6, other arithmetic, local(): g_gate, g_up, g_down, g_in, g_out, g_small = (s.astype(F32) for s in sums)  9.03 us

profile of v2, /device:TPU:27, one launch (start us, length us, event | category | flops | bytes accessed | tf_op | source)
XLA Modules:
  0.0 224.0 jit_solution(16661868534077664699)
XLA Ops:
  0.6 1.2 pad_maximum_fusion.gains
  1.8 124.7 %shard_map.177 = (bf16[8,128,1536]{2,1,0:T(8,128)(2,1)}, bf16[8,128,2304]{2,1,0:T(8,128)(2,1)}, f32[256,1024]{1,0:T(8,128)}, f32[256,1024]{1,0:T(8,128)}, f32[16...) custom-call(bf16[256,1024]{1,0:T(8,128)(2,1)} %bitcast.7, ...), custom_call_target="tpu_custom_call" | custom-call | tf_op jit(solution)/shard_map/pallas_call | solution.py:635
  126.5 85.2 %shard_map.178 = (bf16[128,4608]{1,0:T(8,128)(2,1)}, bf16[128,4608]{1,0:T(8,128)(2,1)}, bf16[128,4608]{1,0:T(8,128)(2,1)}, bf16[128,3072]{1,0:T(8,128)(2,1)}, bf...) custom-call(bf16[2,4,2,4,16,512]{5,4,3,2,1,0:T(8,128)(2,1)} %get-tuple-elem, ...), custom_call_target="tpu_custom_call" | custom-call | tf_op jit(solution)/shard_map/pallas_call | solution.py:1054
  211.7 0.0 copy-start.4
  211.7 0.9 convert_element_type.18
  212.7 0.7 slice_reduce_fusion
  213.4 0.1 slice.23
  213.5 0.7 copy.21
  214.1 0.0 copy-start.2
  214.1 1.9 convert_element_type.20
  216.0 0.0 copy-done.4
  216.0 1.3 convert_element_type.19
  217.3 0.0 copy-done.2
  217.3 0.0 copy-start.1
  217.3 1.6 convert_element_type.21
  219.0 0.0 copy-done.1
  219.0 0.0 copy-start
  219.0 1.6 convert_element_type.22
  220.6 0.0 copy-done
  220.6 0.0 copy-start.5
  220.6 0.0 copy-start.3
  220.6 1.6 convert_element_type.23
  222.3 0.0 copy-done.5
  222.3 0.8 copy.24
  223.0 0.0 copy-done.3
  223.1 1.0 copy.25
  (1 shorter events, 0.0 us)
Async XLA Ops:
  211.7 4.3 %copy-start.4 = (bf16[128,3072]{1,0:T(8,128)(2,1)S(1)}, bf16[128,3072]{1,0:T(8,128)(2,1)}, u32[]{:S(2)}) copy-start(bf16[128,3072]{1,0:T(8,128)(2,1)} %get-tuple-element.93) | copy-start | bytes 2359300
  214.1 3.2 %copy-start.2 = (bf16[128,4608]{1,0:T(8,128)(2,1)S(1)}, bf16[128,4608]{1,0:T(8,128)(2,1)}, u32[]{:S(2)}) copy-start(bf16[128,4608]{1,0:T(8,128)(2,1)} %get-tuple-element.95) | copy-start | bytes 3538948
  217.3 1.6 copy-start.1
  219.0 1.6 copy-start
  220.6 1.6 copy-start.5
  220.6 2.4 %copy-start.3 = (f32[256,1024]{1,0:T(8,128)S(1)}, f32[256,1024]{1,0:T(8,128)}, u32[]{:S(2)}) copy-start(f32[256,1024]{1,0:T(8,128)} %get-tuple-element.91) | copy-start | bytes 3145732

commit v3 on v2

--- a/solution.py
+++ b/solution.py
@@ -486,10 +486,6 @@
     fire(early_copy(2, 1))
     early_fill(2, 1)
     fire(early_copy(2, 2))
-    early_fill(2, 3)
-    fire(early_copy(2, 3))
-    early_fill(2, 0)
-    keep(2)
     stage_c(WDX)
     stage_d(WDZ)
 
@@ -511,6 +507,8 @@
     for t in (0, 1):
         early_fill(t, 1)
         fire(early_copy(t, 2))
+    early_fill(2, 3)
+    fire(early_copy(2, 3))
     swap("mix", part.at[upper], box_mix).wait_send()
 
     def gam_step(j):
@@ -537,7 +535,7 @@
     loop(length // rc, resid_step)
     gmix_swap = swap("gmix", gmix.at[lower], gmix.at[upper])
     gmix_swap.start()
-    for t in (0, 1):
+    for t in (0, 1, 2):
         early_fill(t, 0)
         keep(t)
     gam_swap.wait_send()

time: 226 us -> 225 us (level)
  no operation moved by 1% of the time
where the time goes in v3:
time: 225 us; the launch traced here: 223 us
  Pallas kernels  209 us (93%)
  other arithmetic  10.2 us (5%)
  local copies, waits for them, and re-layouts  3.22 us (1%)
    pallas_call x1, Pallas kernels, block_call(): pl.pallas_call(block_kernel, out_shape=(out(8, rows, 3 * half), out(8, ro...  124 us
    pallas_call x1, Pallas kernels, reduce_grads(): pl.pallas_call(reduce_kernel, out_shape=tuple((jax.ShapeDtypeStruct((rows...  84.8 us
    convert_element_type x6, other arithmetic, local(): g_gate, g_up, g_down, g_in, g_out, g_small = (s.astype(F32) for s in sums)  9.03 us

profile of v3, /device:TPU:27, one launch (start us, length us, event | category | flops | bytes accessed | tf_op | source)
XLA Modules:
  0.0 222.8 jit_solution(14407433114317680123)
XLA Ops:
  0.6 1.2 pad_maximum_fusion.gains
  1.8 123.9 %shard_map.177 = (bf16[8,128,1536]{2,1,0:T(8,128)(2,1)}, bf16[8,128,2304]{2,1,0:T(8,128)(2,1)}, f32[256,1024]{1,0:T(8,128)}, f32[256,1024]{1,0:T(8,128)}, f32[16...) custom-call(bf16[256,1024]{1,0:T(8,128)(2,1)} %bitcast.7, ...), custom_call_target="tpu_custom_call" | custom-call | tf_op jit(solution)/shard_map/pallas_call | solution.py:633
  125.8 84.8 %shard_map.178 = (bf16[128,4608]{1,0:T(8,128)(2,1)}, bf16[128,4608]{1,0:T(8,128)(2,1)}, bf16[128,4608]{1,0:T(8,128)(2,1)}, bf16[128,3072]{1,0:T(8,128)(2,1)}, bf...) custom-call(bf16[2,4,2,4,16,512]{5,4,3,2,1,0:T(8,128)(2,1)} %get-tuple-elem, ...), custom_call_target="tpu_custom_call" | custom-call | tf_op jit(solution)/shard_map/pallas_call | solution.py:1052
  210.5 0.0 copy-start.4
  210.5 0.9 convert_element_type.18
  211.5 0.7 slice_reduce_fusion
  212.2 0.1 slice.23
  212.2 0.7 copy.21
  212.9 0.0 copy-start.2
  212.9 1.9 convert_element_type.20
  214.8 0.0 copy-done.4
  214.8 1.3 convert_element_type.19
  216.1 0.0 copy-done.2
  216.1 0.0 copy-start.1
  216.1 1.6 convert_element_type.21
  217.7 0.0 copy-done.1
  217.7 0.0 copy-start
  217.7 1.6 convert_element_type.22
  219.4 0.0 copy-done
  219.4 0.0 copy-start.5
  219.4 0.0 copy-start.3
  219.4 1.6 convert_element_type.23
  221.0 0.0 copy-done.5
  221.0 0.8 copy.24
  221.8 0.0 copy-done.3
  221.8 1.0 copy.25
  (1 shorter events, 0.0 us)
Async XLA Ops:
  210.5 4.3 %copy-start.4 = (bf16[128,3072]{1,0:T(8,128)(2,1)S(1)}, bf16[128,3072]{1,0:T(8,128)(2,1)}, u32[]{:S(2)}) copy-start(bf16[128,3072]{1,0:T(8,128)(2,1)} %get-tuple-element.93) | copy-start | bytes 2359300
  212.9 3.2 %copy-start.2 = (bf16[128,4608]{1,0:T(8,128)(2,1)S(1)}, bf16[128,4608]{1,0:T(8,128)(2,1)}, u32[]{:S(2)}) copy-start(bf16[128,4608]{1,0:T(8,128)(2,1)} %get-tuple-element.95) | copy-start | bytes 3538948
  216.1 1.6 copy-start.1
  217.7 1.6 copy-start
  219.4 1.6 copy-start.5
  219.4 2.4 %copy-start.3 = (f32[256,1024]{1,0:T(8,128)S(1)}, f32[256,1024]{1,0:T(8,128)}, u32[]{:S(2)}) copy-start(f32[256,1024]{1,0:T(8,128)} %get-tuple-element.91) | copy-start | bytes 3145732
